TPU v7x, 32 devices: a whole 2x2x4 slice. The times are simulated.
32 devices in a mesh: dp: 8 (over z, y), mp: 4 (over x, core).
Axes of the slice: x: 2, y: 2, z: 4, core: 2. Of those that a mesh axis runs over, the one named last changes fastest.
Arguments:
- tokens: bfloat16 [16384, 1024], P(('dp', 'mp')), may hold values from -6 to 6
- counts: int32 [8], P('dp'), may hold values from 1024 to 2048, as said below
- gain_attn: float32 [1024], replicated, may hold values from 0.5 to 1.5
- gain_ffn: float32 [1024], replicated, may hold values from 0.5 to 1.5
- w_qkv: bfloat16 [1024, 3, 1024], P(None, None, 'mp'), may hold values from -0.1875 to 0.1875
- w_out: bfloat16 [1024, 1024], P('mp'), may hold values from -2 to 2
- w_gate_up: bfloat16 [1024, 2, 2816], P(None, None, 'mp'), may hold values from -0.1875 to 0.1875
- w_down: bfloat16 [2816, 1024], P('mp'), may hold values from -0.109375 to 0.109375
- cotangent: bfloat16 [16384, 1024], P(('dp', 'mp')), may hold values from -6 to 6
Outputs:
- latents: float32 [16384, 1024], P(('dp', 'mp'))
- grad_tokens: float32 [16384, 1024], P(('dp', 'mp'))
- grad_gain_attn: float32 [1024], replicated
- grad_gain_ffn: float32 [1024], replicated
- grad_w_qkv: float32 [1024, 3, 1024], P(None, None, 'mp')
- grad_w_out: float32 [1024, 1024], P('mp')
- grad_w_gate_up: float32 [1024, 2, 2816], P(None, None, 'mp')
- grad_w_down: float32 [2816, 1024], P('mp')
Inputs may be any that keep to these rules, and one draw needn't show every extreme that they name: `counts`: number of real patches of each sequence; the rest of its 2048 slots are padding. Some sequence has exactly 2048 and some exactly 1024.
All inputs are finite; a program needn't handle non-finite values.
Results may differ from a plain program's by a relative error of at most 0.015.
Values may be sent and summed in bfloat16 or wider, within the bound.
No kernel may reach another device: no remote copies, remote signals or barrier semaphores. Data moves between devices by JAX's collectives and lax.ppermute only.
A program may use at most 192 MiB of HBM per device.

v0:
```python
import functools

import jax
import jax.numpy as jnp
from jax import lax
from jax.experimental import pallas as pl
from jax.experimental.pallas import tpu as pltpu
from jax.sharding import PartitionSpec as P

HD = 64
EPS = 1e-05
LANES = 128
LOG2E = 1.4426950408889634
NN = (((1,), (0,)), ((), ()))
NT = (((1,), (1,)), ((), ()))
TN = (((0,), (0,)), ((), ()))
f32 = jnp.float32
bf16 = jnp.bfloat16
VMEM_LIMIT = 28 << 20
SHARE = 1


def dot(a, b, dims=NN):
    return lax.dot_general(a, b, dims, preferred_element_type=f32)


def whole(*shape):
    return pl.BlockSpec(shape, lambda *_: (0,) * len(shape))


def smem():
    return pl.BlockSpec(memory_space=pltpu.SMEM)


def shaped(shape, dtype):
    return jax.ShapeDtypeStruct(shape, dtype)


def params():
    return pltpu.CompilerParams(vmem_limit_bytes=VMEM_LIMIT)


def cost(flops, bytes_accessed, transcendentals=0):
    return pl.CostEstimate(
        flops=int(flops * SHARE), bytes_accessed=int(bytes_accessed * SHARE), transcendentals=int(transcendentals * SHARE)
    )


def swap(value, bit, axis="mp"):
    size = lax.axis_size(axis)
    return lax.ppermute(value, axis, [(i, i ^ bit) for i in range(size)])


def after(value, *others):
    return lax.optimization_barrier((value,) + others)[0]


def join(*values):
    return lax.optimization_barrier(values)


def far_of(value):
    return swap(value, 2)


def exchange_rel(parts):
    return [parts[0]] + [swap(parts[k], k) for k in (1, 2, 3)]


def add_low(a, b):
    return (a.astype(f32) + b.astype(f32)).astype(bf16)


def head_lanes(rows, parity):
    lane = lax.broadcasted_iota(jnp.int32, (rows, LANES), 1)
    return (lane // HD) == parity, lane == (1 - parity) * HD


def norm_kernel(x_ref, gain_ref, o_ref):
    x = x_ref[...].astype(f32)
    r = lax.rsqrt(jnp.mean(x * x, axis=1, keepdims=True) + EPS)
    o_ref[...] = (x * r * gain_ref[...]).astype(bf16)


def norm(x, gain):
    rows, width = x.shape
    step = 256
    block = pl.BlockSpec((step, width), lambda i: (i, 0))
    return pl.pallas_call(
        norm_kernel,
        grid=(rows // step,),
        in_specs=[block, whole(1, width)],
        out_specs=block,
        out_shape=shaped((rows, width), bf16),
        compiler_params=params(),
        cost_estimate=cost(rows * width * 8, rows * width * 4),
        name="norm",
    )(x, gain)


def project_kernel(a_ref, b_ref, w_ref, oa_ref, ob_ref):
    cols = w_ref.shape[2]
    for x, o in ((a_ref, oa_ref), (b_ref, ob_ref)):
        for i in range(3):
            o[:, i * cols : (i + 1) * cols] = dot(x[...], w_ref[i]).astype(bf16)


def project(a, b, w):
    rows, width = a.shape
    cols = w.shape[2]
    step = 256
    block = pl.BlockSpec((step, width), lambda i: (i, 0))
    block_out = pl.BlockSpec((step, 3 * cols), lambda i: (i, 0))
    return pl.pallas_call(
        project_kernel,
        grid=(rows // step,),
        in_specs=[block, block, whole(3, width, cols)],
        out_specs=[block_out, block_out],
        out_shape=[shaped((rows, 3 * cols), bf16)] * 2,
        compiler_params=params(),
        cost_estimate=cost(12 * rows * width * cols, 4 * rows * (width + 3 * cols)),
        name="project",
    )(a, b, w)


def attn_fwd_kernel(me_ref, count_ref, p0_ref, p1_ref, n2_ref, n3_ref, w_ref, qkv_ref, o_ref, lse_ref, a0_ref, a1_ref, a2_ref, a3_ref, kaug, *, length, columns, block):
    h = pl.program_id(0)
    rows_each = length // 4
    me = me_ref[0]

    def spot(k):
        return pl.ds(pl.multiple_of((me ^ k) * rows_each, rows_each), rows_each)

    @pl.when(h == 0)
    def _():
        qkv_ref[spot(0), :] = p0_ref[...]
        qkv_ref[spot(1), :] = p1_ref[...]
        for k, n in ((2, n2_ref), (3, n3_ref)):
            for i in range(3):
                qkv_ref[spot(k), i * columns : (i + 1) * columns] = dot(n[...], w_ref[i]).astype(bf16)

    parity = lax.rem(h, 2)
    col = pl.multiple_of((h // 2) * LANES, LANES)
    c = HD**-0.5 * LOG2E
    sel, spare = head_lanes(length, parity)
    row = lax.broadcasted_iota(jnp.int32, (length, LANES), 0)
    k = qkv_ref[:, pl.ds(columns + col, LANES)].astype(f32)
    bias = jnp.where(row < count_ref[0], 0.0, -1e30)
    kaug[...] = jnp.where(sel, k, jnp.where(spare, bias, 0.0)).astype(bf16)
    sel_b, spare_b = head_lanes(block, parity)
    ri = lax.broadcasted_iota(jnp.int32, (block, block), 0)
    ci = lax.broadcasted_iota(jnp.int32, (block, block), 1)
    for i in range(length // block):
        first = i * block
        n = first + block
        rows = pl.ds(first, block)
        q = qkv_ref[rows, pl.ds(col, LANES)].astype(f32)
        q = jnp.where(sel_b, q, jnp.where(spare_b, 1.0, 0.0)).astype(bf16)
        s_d = dot(q, kaug[first:n], NT)
        s_d = jnp.where(ci <= ri, s_d, -1e30)
        m = jnp.max(s_d, axis=1, keepdims=True)
        if first:
            s_o = dot(q, kaug[:first], NT)
            m = jnp.maximum(m, jnp.max(s_o, axis=1, keepdims=True))
        mc = m * c
        p_d = jnp.exp2(s_d * c - mc)
        total = jnp.sum(p_d, axis=1, keepdims=True)
        o = dot(p_d.astype(bf16), qkv_ref[first:n, pl.ds(2 * columns + col, LANES)])
        if first:
            p_o = jnp.exp2(s_o * c - mc)
            total = total + jnp.sum(p_o, axis=1, keepdims=True)
            o = o + dot(p_o.astype(bf16), qkv_ref[:first, pl.ds(2 * columns + col, LANES)])
        o = (o / total).astype(bf16)
        out = pl.ds(col, LANES)
        o_ref[rows, out] = jnp.where(sel_b, o, o_ref[rows, out])
        lse = mc + jnp.log2(total)
        lse_ref[pl.ds(h, 1), first:n] = jnp.transpose(jnp.broadcast_to(lse, (block, LANES)))[0:1]

    @pl.when(h == pl.num_programs(0) - 1)
    def _():
        for k, ref in enumerate((a0_ref, a1_ref, a2_ref, a3_ref)):
            ref[...] = o_ref[spot(k), :]


def attn_fwd(me, count, p0, p1, n2, n3, w, block=512):
    each, width = n2.shape
    length = 4 * each
    columns = w.shape[2]
    three = 3 * columns
    heads = columns // HD
    return pl.pallas_call(
        functools.partial(attn_fwd_kernel, length=length, columns=columns, block=block),
        grid=(heads,),
        out_shape=[shaped((length, three), bf16), shaped((length, columns), bf16), shaped((heads, length), f32)]
        + [shaped((each, columns), bf16)] * 4,
        in_specs=[smem(), smem(), whole(each, three), whole(each, three), whole(each, width), whole(each, width), whole(3, width, columns)],
        out_specs=[whole(length, three), whole(length, columns), whole(heads, length)] + [whole(each, columns)] * 4,
        scratch_shapes=[pltpu.VMEM((length, LANES), bf16)],
        compiler_params=params(),
        cost_estimate=cost(10 * length * length * columns, 2 * length * columns * 8, length * length * heads // 2),
        name="attn_fwd",
    )(me, count, p0, p1, n2, n3, w)


def attn_bwd_kernel(me_ref, count_ref, q_ref, k_ref, v_ref, d0_ref, d1_ref, d2_ref, d3_ref, o_ref, lse_ref, *rest, length, block, pair):
    g_ref, do_all, kaug, qaug, dom, dq = rest[-6:]
    parity = pl.program_id(0)
    rows_each = length // 4
    me = me_ref[0]

    @pl.when(parity == 0)
    def _():
        for k, ref in enumerate((d0_ref, d1_ref, d2_ref, d3_ref)):
            do_all[pl.ds(pl.multiple_of((me ^ k) * rows_each, rows_each), rows_each), :] = ref[...]

    scale = HD**-0.5
    c = scale * LOG2E
    sel, spare = head_lanes(length, parity)
    row = lax.broadcasted_iota(jnp.int32, (length, LANES), 0)
    bias = jnp.where(row < count_ref[0], 0.0, -1e30)
    kaug[...] = jnp.where(sel, k_ref[...].astype(f32), jnp.where(spare, bias, 0.0)).astype(bf16)
    qaug[...] = jnp.where(sel, q_ref[...].astype(f32), jnp.where(spare, 1.0, 0.0)).astype(bf16)
    do = jnp.where(sel, do_all[...].astype(f32), 0.0)
    dom[...] = do.astype(bf16)
    prod = do * o_ref[...].astype(f32)
    hi = prod.astype(bf16)
    lo = (prod - hi.astype(f32)).astype(bf16)
    ones = jnp.ones((8, LANES), bf16)
    delta = (dot(ones, hi, NT) + dot(ones, lo, NT))[0:1]
    lse = lse_ref[pl.ds(2 * pair + parity, 1), :]
    sel_b, _ = head_lanes(block, parity)
    ki = lax.broadcasted_iota(jnp.int32, (block, block), 0)
    qi = lax.broadcasted_iota(jnp.int32, (block, block), 1)
    dq[...] = jnp.zeros_like(dq)
    for j in range(length // block):
        first = j * block
        last = first + block
        kj = kaug[first:last]
        vj = v_ref[first:last]

        def part(a, b, diag):
            s = dot(kj, qaug[a:b], NT)
            if diag:
                s = jnp.where(ki <= qi, s, -1e30)
            p = jnp.exp2(s * c - lse[:, a:b])
            dp = dot(vj, dom[a:b], NT)
            ds = (p * (dp - delta[:, a:b])).astype(bf16)
            dv = dot(p.astype(bf16), dom[a:b])
            dk = dot(ds, qaug[a:b])
            dq[a:b] += dot(ds, kj, TN)
            return dv, dk

        dv, dk = part(first, last, True)
        if last < length:
            dv2, dk2 = part(last, length, False)
            dv = dv + dv2
            dk = dk + dk2
        for idx, val in ((1, dk * scale), (2, dv)):
            out = slice(idx * LANES, (idx + 1) * LANES)
            g_ref[first:last, out] = jnp.where(sel_b, val.astype(bf16), g_ref[first:last, out])
    g_ref[:, :LANES] = jnp.where(sel, (dq[...] * scale).astype(bf16), g_ref[:, :LANES])


def attn_bwd(me, count, qkv, d_list, o, lse, pair, deps=(), block=512):
    length, three = qkv.shape
    columns = three // 3
    heads = columns // HD
    pairs = columns // LANES
    each = length // 4

    def part(rows, col):
        return pl.BlockSpec((rows, LANES), lambda i: (0, col))

    return pl.pallas_call(
        functools.partial(attn_bwd_kernel, length=length, block=block, pair=pair),
        grid=(2,),
        out_shape=shaped((length, 3 * LANES), bf16),
        in_specs=[smem(), smem()]
        + [part(length, i * pairs + pair) for i in range(3)]
        + [part(each, pair)] * 4
        + [part(length, pair), whole(heads, length)]
        + [pl.BlockSpec(memory_space=pl.ANY)] * len(deps),
        out_specs=whole(length, 3 * LANES),
        scratch_shapes=[pltpu.VMEM((length, LANES), bf16)] * 4 + [pltpu.VMEM((length, LANES), f32)],
        compiler_params=params(),
        cost_estimate=cost(20 * length * length * LANES, 2 * length * LANES * 8, length * length),
        name="attn_bwd",
    )(me, count, qkv, qkv, qkv, *d_list, o, lse, *deps)


def middle_kernel(x_ref, a0, a1, a2, a3, w0, w1, w2, w3, gain_ref, mid_ref, normed_ref):
    total = x_ref[...].astype(f32)
    acc = dot(a0[...], w0[...]) + dot(a1[...], w1[...]) + dot(a2[...], w2[...]) + dot(a3[...], w3[...])
    total = total + acc
    mid_ref[...] = total
    r = lax.rsqrt(jnp.mean(total * total, axis=1, keepdims=True) + EPS)
    normed_ref[...] = (total * r * gain_ref[...]).astype(bf16)


def middle_of(tokens, a_list, w_list, gain):
    rows, width = tokens.shape
    cols = a_list[0].shape[1]
    step = 256
    block = pl.BlockSpec((step, width), lambda i: (i, 0))
    block_a = pl.BlockSpec((step, cols), lambda i: (i, 0))
    return pl.pallas_call(
        middle_kernel,
        grid=(rows // step,),
        in_specs=[block] + [block_a] * 4 + [whole(cols, width)] * 4 + [whole(1, width)],
        out_specs=[block, block],
        out_shape=[shaped((rows, width), f32), shaped((rows, width), bf16)],
        compiler_params=params(),
        cost_estimate=cost(2 * rows * width * width, rows * width * 10 + 2 * width * width),
        name="middle",
    )(tokens, *a_list, *w_list, gain)


def ffn_kernel(na, nb, ca, cb, w, wd, hid_ref, gg_ref, gu_ref, pda, pdb, pga, pgb, xs, cs, *, half):
    i = pl.program_id(0)

    @pl.when(i < half)
    def _():
        xs[...] = na[...]
        cs[...] = ca[...]

    @pl.when(i >= half)
    def _():
        xs[...] = nb[...]
        cs[...] = cb[...]

    x = xs[...]
    gate = dot(x, w[0], NT)
    up = dot(x, w[1], NT)
    grad_hidden = dot(cs[...], wd[...], NT)
    sig = jax.nn.sigmoid(gate)
    silu = gate * sig
    hidden = (silu * up).astype(bf16)
    hid_ref[...] = hidden
    gg = (grad_hidden * up * (sig * (1.0 + gate * (1.0 - sig)))).astype(bf16)
    gu = (grad_hidden * silu).astype(bf16)
    gg_ref[...] = gg
    gu_ref[...] = gu
    down = dot(hidden, wd[...]).astype(bf16)
    grad_normed = (dot(gg, w[0]) + dot(gu, w[1])).astype(bf16)

    @pl.when(i < half)
    def _():
        pda[...] = down
        pga[...] = grad_normed

    @pl.when(i >= half)
    def _():
        pdb[...] = down
        pgb[...] = grad_normed


def ffn(na, nb, ca, cb, w, wd):
    rows, width = na.shape
    hid = wd.shape[0]
    step = 256
    half = rows // step
    first = pl.BlockSpec((step, width), lambda i: (jnp.minimum(i, half - 1), 0))
    second = pl.BlockSpec((step, width), lambda i: (jnp.maximum(i - half, 0), 0))
    block_h = pl.BlockSpec((step, hid), lambda i: (i, 0))
    return pl.pallas_call(
        functools.partial(ffn_kernel, half=half),
        grid=(2 * half,),
        in_specs=[first, second, first, second, whole(2, hid, width), whole(hid, width)],
        out_specs=[block_h] * 3 + [first, second] * 2,
        out_shape=[shaped((2 * rows, hid), bf16)] * 3 + [shaped((rows, width), bf16)] * 4,
        scratch_shapes=[pltpu.VMEM((step, width), bf16)] * 2,
        compiler_params=params(),
        cost_estimate=cost(24 * rows * width * hid, 12 * rows * (width + hid), 2 * rows * hid),
        name="ffn",
    )(na, nb, ca, cb, w, wd)


def grad_middle_kernel(cot, mid, g0, g1, g2, gain, w0, w1, w2, w3, gm_ref, gml_ref, o0, o1, o2, o3):
    dn = g0[...].astype(f32) + g1[...].astype(f32) + g2[...].astype(f32)
    x = mid[...]
    r = lax.rsqrt(jnp.mean(x * x, axis=1, keepdims=True) + EPS)
    e = dn * gain[...]
    gm = cot[...].astype(f32) + r * e - x * (r * r * r * jnp.mean(e * x, axis=1, keepdims=True))
    gm_ref[...] = gm
    low = gm.astype(bf16)
    gml_ref[...] = low
    for w, o in ((w0, o0), (w1, o1), (w2, o2), (w3, o3)):
        o[...] = dot(low, w[...], NT).astype(bf16)


def grad_middle_of(cot, mid, parts, gain, w_list):
    rows, width = cot.shape
    cols = w_list[0].shape[0]
    step = 256
    block = pl.BlockSpec((step, width), lambda i: (i, 0))
    block_a = pl.BlockSpec((step, cols), lambda i: (i, 0))
    return pl.pallas_call(
        grad_middle_kernel,
        grid=(rows // step,),
        in_specs=[block] * 5 + [whole(1, width)] + [whole(cols, width)] * 4,
        out_specs=[block, block] + [block_a] * 4,
        out_shape=[shaped((rows, width), f32), shaped((rows, width), bf16)] + [shaped((rows, cols), bf16)] * 4,
        compiler_params=params(),
        cost_estimate=cost(2 * rows * width * width, rows * width * 20 + 2 * width * width),
        name="grad_middle",
    )(cot, mid, *parts, gain, *w_list)


def grad_tokens_kernel(gm, tok, g0, g1, g2, gain, out_ref):
    dn = g0[...].astype(f32) + g1[...].astype(f32) + g2[...].astype(f32)
    x = tok[...].astype(f32)
    r = lax.rsqrt(jnp.mean(x * x, axis=1, keepdims=True) + EPS)
    e = dn * gain[...]
    out_ref[...] = gm[...] + r * e - x * (r * r * r * jnp.mean(e * x, axis=1, keepdims=True))


def grad_tokens_of(gm, tokens, parts, gain):
    rows, width = gm.shape
    step = 256
    block = pl.BlockSpec((step, width), lambda i: (i, 0))
    return pl.pallas_call(
        grad_tokens_kernel,
        grid=(rows // step,),
        in_specs=[block] * 5 + [whole(1, width)],
        out_specs=block,
        out_shape=shaped((rows, width), f32),
        compiler_params=params(),
        cost_estimate=cost(rows * width * 20, rows * width * 20),
        name="grad_tokens",
    )(gm, tokens, *parts, gain)


def qkv_dgrad_kernel(me_ref, g0_ref, g1_ref, w_ref, oa_ref, ob_ref, *, ka, kb):
    each = oa_ref.shape[0]
    me = me_ref[0]
    for k, o in ((ka, oa_ref), (kb, ob_ref)):
        rows = pl.ds(pl.multiple_of((me ^ k) * each, each), each)
        total = None
        for i in range(3):
            cols = slice(i * LANES, (i + 1) * LANES)
            g = jnp.concatenate([g0_ref[rows, cols], g1_ref[rows, cols]], axis=1)
            term = dot(g, w_ref[i], NT)
            total = term if total is None else total + term
        o[...] = total.astype(bf16)


def qkv_dgrad(me, g0, g1, w, ka, kb):
    length, three = g0.shape
    width = w.shape[1]
    each = length // 4
    vm = pl.BlockSpec(memory_space=pltpu.VMEM)
    return pl.pallas_call(
        functools.partial(qkv_dgrad_kernel, ka=ka, kb=kb),
        in_specs=[smem()] + [vm] * 3,
        out_specs=[vm] * 2,
        out_shape=[shaped((each, width), bf16)] * 2,
        compiler_params=params(),
        cost_estimate=cost(8 * each * width * three, 2 * (2 * length * three + 2 * width * three + 2 * each * width)),
        name="qkv_dgrad",
    )(me, g0, g1, w)


def block_of(y, z, me):
    return (2 * z + y) ^ me


def spot_of(y, z, lead):
    if lead == "y":
        return y, (z & 1) * 2 + (z >> 1)
    return z & 1, y * 2 + (z >> 1)


def wgrad_cols_kernel(dp_ref, ha, hb, c0, c1, c2, c3, *rest, each, lead):
    acc = rest[-1]
    halves = rest[-3:-1]
    acc[...] = dot(ha[:each], c0[...], TN)
    acc[...] += dot(ha[each:], c1[...], TN)
    acc[...] += dot(hb[:each], c2[...], TN)
    acc[...] += dot(hb[each:], c3[...], TN)
    wide = halves[0].shape[2]
    for z in range(4):
        for y in range(2):
            b = block_of(y, z, dp_ref[0])
            half, spot = spot_of(y, z, lead)
            halves[half][spot] = acc[:, pl.ds(pl.multiple_of(b * wide, wide), wide)].astype(bf16)


def wgrad_cols(dp, ha, hb, c_list, lead="y"):
    hid = ha.shape[1]
    each, width = c_list[0].shape
    vm = pl.BlockSpec(memory_space=pltpu.VMEM)
    return pl.pallas_call(
        functools.partial(wgrad_cols_kernel, each=each, lead=lead),
        in_specs=[smem()] + [vm] * 6,
        out_specs=[vm] * 2,
        out_shape=[shaped((4, hid, width // 8), bf16)] * 2,
        scratch_shapes=[pltpu.VMEM((hid, width), f32)],
        compiler_params=params(),
        cost_estimate=cost(8 * each * width * hid, 8 * each * (width + hid) + 2 * width * hid),
        name="wgrad_cols",
    )(dp, ha, hb, *c_list)


def wgrad_out_kernel(gml, a0, a1, a2, a3, o0, o1, o2, o3):
    for a, o in ((a0, o0), (a1, o1), (a2, o2), (a3, o3)):
        o[...] = dot(a[...], gml[...], TN).astype(bf16)


def wgrad_out(gml, a_list):
    each, width = gml.shape
    cols = a_list[0].shape[1]
    vm = pl.BlockSpec(memory_space=pltpu.VMEM)
    return pl.pallas_call(
        wgrad_out_kernel,
        in_specs=[vm] * 5,
        out_specs=[vm] * 4,
        out_shape=[shaped((cols, width), bf16)] * 4,
        compiler_params=params(),
        cost_estimate=cost(8 * each * width * cols, 4 * each * width + 2 * width * width),
        name="wgrad_out",
    )(gml, *a_list)


def wgrad_qkv_kernel(me_ref, dp_ref, g_ref, n0, n1, n2, n3, *rest, each):
    keep_ref, send_ref, acc = rest[-3:]
    me = me_ref[0]
    for k, n in enumerate((n0, n1, n2, n3)):
        rows = pl.ds(pl.multiple_of((me ^ k) * each, each), each)
        term = dot(n[...], g_ref[rows, :], TN)
        if k:
            acc[...] += term
        else:
            acc[...] = term
    tall = keep_ref.shape[1]
    three = g_ref.shape[1]
    for z in range(4):
        for y in range(2):
            b = block_of(y, z, dp_ref[0])
            half, spot = spot_of(y, z, "y")
            o = (keep_ref, send_ref)[half]
            rows = pl.ds(pl.multiple_of(b * tall, tall), tall)
            o[spot, :, :three] = acc[rows, :].astype(bf16)
            if len(rest) > 3:
                out = rest[0][:, rows].astype(f32) + rest[1][:, rows].astype(f32) + rest[2][:, rows].astype(f32)
                for i in range(out.shape[0] // tall):
                    o[spot, :, three + i * tall : three + (i + 1) * tall] = out[i * tall : (i + 1) * tall].astype(bf16)


def wgrad_qkv(me, dp, grad, n_list, w_parts=()):
    length, three = grad.shape
    each, width = n_list[0].shape
    extra = w_parts[0].shape[0] if w_parts else 0
    vm = pl.BlockSpec(memory_space=pltpu.VMEM)
    return pl.pallas_call(
        functools.partial(wgrad_qkv_kernel, each=each),
        in_specs=[smem(), smem()] + [vm] * (5 + len(w_parts)),
        out_specs=[vm] * 2,
        out_shape=[shaped((4, width // 8, three + extra), bf16)] * 2,
        scratch_shapes=[pltpu.VMEM((width, three), f32)],
        compiler_params=params(),
        cost_estimate=cost(2 * length * width * three, 2 * length * (width + three) + 2 * width * (three + 4 * extra)),
        name="wgrad_qkv",
    )(me, dp, grad, *n_list, *w_parts)


def add_split_kernel(a_ref, b_ref, o0, o1):
    half = o0.shape[0]
    o0[...] = (a_ref[:half].astype(f32) + b_ref[:half].astype(f32)).astype(bf16)
    o1[...] = (a_ref[half:].astype(f32) + b_ref[half:].astype(f32)).astype(bf16)


def add_split(a, b):
    vm = pl.BlockSpec(memory_space=pltpu.VMEM)
    half = (a.shape[0] // 2,) + a.shape[1:]
    return pl.pallas_call(
        add_split_kernel,
        in_specs=[vm] * 2,
        out_specs=[vm] * 2,
        out_shape=[shaped(half, bf16)] * 2,
        compiler_params=params(),
        cost_estimate=cost(a.size, 6 * a.size),
        name="add_split",
    )(a, b)


class Chain:
    def __init__(self, kept, sent, lead="y"):
        self.single = lax.axis_size("dp") != 8
        self.steps = 0
        self.kept = kept
        if self.single:
            self.parts = (lax.psum(kept, "dp"), lax.psum(sent, "dp"))
            return
        self.bits = (1, 2, 4, 2, 1) if lead == "y" else (2, 1, 4, 1, 2)
        self.flying = swap(sent, self.bits[0], "dp")

    def close(self, *others):
        if self.single:
            return (self.kept,)
        self.flying = join(self.flying, *others)[0]
        return (self.flying,)

    def step(self, *others):
        if self.single:
            return (self.kept,)
        self.steps += 1
        got = join(self.flying, *others)[0]
        if self.steps == 1:
            self.kept, sent = add_split(self.kept, got)
        elif self.steps == 2:
            self.kept = sent = add_low(self.kept, got)
        elif self.steps == 3:
            self.kept = sent = add_low(self.kept, got[::-1])
        elif self.steps == 4:
            self.kept = sent = jnp.concatenate([self.kept, got], axis=0)
        else:
            self.parts = (self.kept, got)
            return (got,)
        self.flying = swap(sent, self.bits[self.steps], "dp")
        return (sent,)

    def finish(self, *others):
        while not self.single and self.steps < 5:
            self.step(*others)
        return self.parts


def pieces(refs, lead="y"):
    for y in range(2):
        for z in range(4):
            half, spot = spot_of(y, z, lead)
            yield y, z, refs[half], spot


def finish_down_kernel(dp_ref, k_ref, s_ref, o_ref):
    wide = k_ref.shape[2]
    for y, z, ref, spot in pieces((k_ref, s_ref)):
        cols = pl.ds(pl.multiple_of(block_of(y, z, dp_ref[0]) * wide, wide), wide)
        o_ref[:, cols] = ref[spot].astype(f32)


def finish_down(dp, parts, shape):
    vm = pl.BlockSpec(memory_space=pltpu.VMEM)
    return pl.pallas_call(
        finish_down_kernel,
        in_specs=[smem()] + [vm] * 2,
        out_specs=vm,
        out_shape=shaped(shape, f32),
        compiler_params=params(),
        cost_estimate=cost(shape[0] * shape[1], 6 * shape[0] * shape[1]),
        name="finish_down",
    )(dp, *parts)


def finish_cols_kernel(dp_ref, k_ref, s_ref, w_ref, gain_ref, *rest, lead):
    o_ref, part_ref = rest[-2:]
    wide = k_ref.shape[2]
    for y, z, ref, spot in pieces((k_ref, s_ref), lead):
        cols = pl.ds(pl.multiple_of(block_of(y, z, dp_ref[0]) * wide, wide), wide)
        grad = ref[spot].astype(f32)
        o_ref[0, :, cols] = grad
        part_ref[:, cols] = jnp.sum(grad * w_ref[0, :, cols].astype(f32), axis=0, keepdims=True) / gain_ref[:, cols]


def finish_cols(dp, parts, w, gain, index, into=None, lead="y"):
    two, hid, width = w.shape
    one = pl.BlockSpec((1, hid, width), lambda i: (index, 0, 0))
    extra = () if into is None else (into,)
    return pl.pallas_call(
        functools.partial(finish_cols_kernel, lead=lead),
        grid=(1,),
        in_specs=[smem(), whole(*parts[0].shape), whole(*parts[1].shape), one, whole(1, width)] + [pl.BlockSpec(memory_space=pl.ANY)] * len(extra),
        out_specs=[one, whole(1, width)],
        out_shape=[shaped(w.shape, f32), shaped((1, width), f32)],
        input_output_aliases={5: 0} if extra else {},
        compiler_params=params(),
        cost_estimate=cost(4 * hid * width, 8 * hid * width),
        name="finish_cols",
    )(dp, *parts, w, gain, *extra)


def half_gain_kernel(dp_ref, a_ref, b_ref, w_ref, gain_ref, o_ref, *, y):
    tall = a_ref.shape[1]
    o_ref[...] = jnp.zeros_like(o_ref)
    for z in range(4):
        _, spot = spot_of(y, z, "y")
        rows = pl.ds(pl.multiple_of(block_of(y, z, dp_ref[0]) * tall, tall), tall)
        total = None
        for idx in range(3):
            part = slice(idx * LANES, (idx + 1) * LANES)
            for pair, ref in enumerate((a_ref, b_ref)):
                term = ref[spot, :, part].astype(f32) * w_ref[idx, rows, pair * LANES : (pair + 1) * LANES].astype(f32)
                total = term if total is None else total + term
        total = jnp.sum(total, axis=1, keepdims=True)
        o_ref[:, rows] = jnp.transpose(jnp.broadcast_to(total, (tall, LANES)))[0:1] / gain_ref[:, rows]


def half_gain(dp, first, second, w, gain, y):
    vm = pl.BlockSpec(memory_space=pltpu.VMEM)
    width = w.shape[1]
    return pl.pallas_call(
        functools.partial(half_gain_kernel, y=y),
        in_specs=[smem()] + [vm] * 4,
        out_specs=vm,
        out_shape=shaped((1, width), f32),
        compiler_params=params(),
        cost_estimate=cost(2 * w.size, 4 * w.size),
        name="half_gain",
    )(dp, first, second, w, gain)


def finish_qkv_kernel(dp_ref, ak, sk, bk, bs, o_ref, out_ref):
    tall = ak.shape[1]
    cols = out_ref.shape[0]
    three = 3 * LANES
    for (y, z, a, spot), (_, _, b, _) in zip(pieces((ak, sk)), pieces((bk, bs))):
        rows = pl.ds(pl.multiple_of(block_of(y, z, dp_ref[0]) * tall, tall), tall)
        for idx in range(3):
            part = slice(idx * LANES, (idx + 1) * LANES)
            o_ref[idx, rows, :LANES] = a[spot, :, part].astype(f32)
            o_ref[idx, rows, LANES:] = b[spot, :, part].astype(f32)
        for k in range(cols // tall):
            out_ref[k * tall : (k + 1) * tall, rows] = a[spot, :, three + k * tall : three + (k + 1) * tall].astype(f32)


def finish_qkv(dp, first, second, cols):
    vm = pl.BlockSpec(memory_space=pltpu.VMEM)
    width = 8 * first[0].shape[1]
    return pl.pallas_call(
        finish_qkv_kernel,
        in_specs=[smem()] + [vm] * 4,
        out_specs=[vm] * 2,
        out_shape=[shaped((3, width, cols), f32), shaped((cols, width), f32)],
        compiler_params=params(),
        cost_estimate=cost(8 * cols * width, 24 * cols * width),
        name="finish_qkv",
    )(dp, *first, *second)


def on_device(tokens, counts, gain_attn, gain_ffn, w_qkv, w_out, w_gate_up, w_down, cotangent):
    rows, width = tokens.shape
    columns = w_qkv.shape[2]
    hid = w_gate_up.shape[2]
    me = lax.axis_index("mp").astype(jnp.int32).reshape(1)
    dp = jnp.zeros((1,), jnp.int32)
    if lax.axis_size("dp") == 8:
        dp = lax.axis_index("dp").astype(jnp.int32).reshape(1)
    gain_a = gain_attn.reshape(1, width)
    gain_f = gain_ffn.reshape(1, width)
    qkv_w = jnp.transpose(w_qkv, (1, 0, 2))
    gate_up_w = jnp.transpose(w_gate_up, (1, 2, 0))

    n0 = norm(tokens, gain_a)
    n2 = far_of(n0)
    n1 = swap(n0, 1)
    p0, p1 = project(n0, n1, qkv_w)
    n2, p0, p1 = join(n2, p0, p1)
    n = [n0, n1, n2, swap(n2, 1)]
    out2 = far_of(after(w_out, n2))
    cot2 = far_of(after(cotangent, *n[2:]))
    qkv, attended, lse, *a = attn_fwd(me, counts, p0, p1, n[2], n[3], qkv_w)
    out2, *a = join(out2, *a)
    out_w = [w_out, swap(w_out, 1), out2, swap(out2, 1)]
    a = exchange_rel(a)
    cot2, *a = join(cot2, *a)
    cot = [cotangent, swap(cotangent, 1), cot2, swap(cot2, 1)]
    middle, m0 = middle_of(tokens, a, out_w, gain_f)
    m2 = far_of(m0)
    m1 = swap(m0, 1)
    hid_a, gg_a, gu_a, d0, d1, g0, g1 = ffn(m0, m1, cot[0], cot[1], gate_up_w, w_down)
    m2, hid_a, gg_a, gu_a, d0, d1, g0, g1 = join(m2, hid_a, gg_a, gu_a, d0, d1, g0, g1)
    m = [m0, m1, m2, swap(m2, 1)]
    g1, d1 = swap(g1, 1), swap(d1, 1)
    hid_b, gg_b, gu_b, d2, d3, g2, g3 = ffn(m[2], m[3], cot[2], cot[3], gate_up_w, w_down)
    g1, d1, g2, g3 = join(g1, d1, g2, g3)
    sent = add_low(g2, swap(g3, 1))
    s2 = far_of(sent)
    d3 = swap(after(d3, sent), 1)
    down = Chain(*wgrad_cols(dp, after(hid_a, sent), hid_b, cot))
    parts = wgrad_cols(dp, after(gu_a, down.kept), gu_b, m)
    up = Chain(*parts)
    parts = wgrad_cols(dp, after(gg_a, up.kept), gg_b, m, "z")
    gate_kept, gate_sent = parts
    lat_sent = add_low(d2, d3)
    x = down.step(gate_kept)
    s2 = join(s2, lat_sent, *x)[0]
    grad_middle, low, *ga = grad_middle_of(cotangent, middle, (g0, g1, s2), gain_f, out_w)
    d_list = exchange_rel(ga)
    gate = Chain(gate_kept, after(gate_sent, low), "z")
    w0, w1, w2, w3 = wgrad_out(low, a)
    x = up.step(w0) + down.step(w0)
    d_list = join(*d_list, *x)[:4]
    w1, w3 = join(swap(w1, 1), swap(w3, 1), *d_list)[:2]
    w_sent = add_low(w2, w3)
    w2 = far_of(w_sent)
    grad0 = attn_bwd(me, counts, qkv, d_list, attended, lse, 0, (w_sent,))
    w2 = join(w2, grad0)[0]
    x = down.step(grad0) + up.step(grad0) + gate.step(grad0)
    parts = wgrad_qkv(me, dp, after(grad0, *x), n, (w0, w1, w2))
    first = Chain(*parts)
    lat2 = far_of(after(lat_sent, first.kept))
    grad1 = attn_bwd(me, counts, qkv, d_list, attended, lse, 1, (first.kept,))
    x = down.step(grad1) + up.step(grad1) + gate.step(grad1) + first.close(grad1) + (lat2,)
    t2, t3 = qkv_dgrad(me, grad0, after(grad1, *x), qkv_w, 2, 3)
    t3 = swap(t3, 1)
    t0, t1 = qkv_dgrad(me, grad0, after(grad1, t2), qkv_w, 0, 1)
    t3 = join(t3, t0)[0]
    sent = add_low(t2, t3)
    t2 = far_of(sent)
    x = first.step(sent)
    parts = wgrad_qkv(me, dp, after(grad1, *x), n)
    second = Chain(*parts)
    latents = middle + d0.astype(f32) + d1.astype(f32) + after(lat2, second.kept).astype(f32)
    t1 = swap(after(t1, latents), 1)
    x = up.step(latents)
    x = first.step(*x)
    x = gate.step(*x)
    x = second.step(*x)
    grad_w_down = finish_down(dp, down.finish(*x), (hid, width))
    x = first.step(grad_w_down)
    x = second.step(*x)
    t0, t1, t2 = join(t0, t1, t2, *x)[:3]
    grad_tokens = grad_tokens_of(grad_middle, tokens, (t0, t1, t2), gain_a)
    x = first.step(grad_tokens)
    x = second.step(*x)
    grad_w_gate_up, part_u = finish_cols(dp, up.finish(*x), gate_up_w, gain_f, 1)
    x = second.step(grad_w_gate_up)
    if lax.axis_size("dp") == 8:
        gain_1 = half_gain(dp, first.kept, after(second.kept, *x), qkv_w, gain_a, 0)
        gain_1 = gain_1 + swap(gain_1, 1) + swap(gain_1, 2) + swap(gain_1, 3)
        gain_1 = gain_1 + swap(gain_1, 1, "dp")
    else:
        parts = [half_gain(dp, first.parts[y], second.parts[y], qkv_w, gain_a, y) for y in range(2)]
        gain_1 = parts[0] + parts[1]
        gain_1 = gain_1 + swap(gain_1, 1) + swap(gain_1, 2) + swap(gain_1, 3)
    grad_w_gate_up, part_g = finish_cols(dp, gate.finish(*x), gate_up_w, gain_f, 0, grad_w_gate_up, "z")
    gain_2 = part_u + part_g
    gain_2 = gain_2 + swap(gain_2, 1) + swap(gain_2, 2) + swap(gain_2, 3)
    grad_w_qkv, grad_w_out = finish_qkv(dp, first.finish(grad_w_gate_up), second.finish(grad_w_gate_up), columns)
    gains = (gain_1, gain_2)
    grad_w_qkv = jnp.transpose(grad_w_qkv, (1, 0, 2))
    grad_w_gate_up = jnp.transpose(grad_w_gate_up, (2, 0, 1))
    return (
        latents,
        grad_tokens,
        gains[0].reshape(width),
        gains[1].reshape(width),
        grad_w_qkv,
        grad_w_out,
        grad_w_gate_up,
        grad_w_down,
    )


def solution(mesh):
    placed = (
        P(("dp", "mp"), None),
        P("dp"),
        P(),
        P(),
        P(None, None, "mp"),
        P("mp", None),
        P(None, None, "mp"),
        P("mp", None),
        P(("dp", "mp"), None),
    )
    return jax.shard_map(
        on_device,
        mesh=mesh,
        in_specs=placed,
        out_specs=(
            P(("dp", "mp"), None),
            P(("dp", "mp"), None),
            P(),
            P(),
            P(None, None, "mp"),
            P("mp", None),
            P(None, None, "mp"),
            P("mp", None),
        ),
        check_vma=False,
    )
```

profile of v0, /device:TPU:0, one launch (start us, length us, event | category | flops | bytes accessed | tf_op | source)
XLA Modules:
  0.0 357.0 jit_solution(12930398645413001038)
XLA Ops:
  9.9 20.0 %collective-permute-done.n2_ref.n2 = bf16[512,1024]{1,0:T(8,128)(2,1)S(1)} collective-permute-done((bf16[512,1024]{1,0:T(8,128)(2,1)S(1)}, bf16[512,1024]{1,0:T(8,128)(2,1)S(1)}, u32[]{:S(2)}, u32[]{:S(2)}) %collective-permute-start) | collective-permute-done | bytes 1048608 | tf_op jit(solution)/shard_map/ppermute | solution.py:51
  36.7 22.1 %attn_fwd.1 = (bf16[2048,768]{1,0:T(8,128)(2,1)S(1)}, bf16[2048,256]{1,0:T(8,128)(2,1)S(1)}, f32[4,2048]{1,0:T(4,128)S(1)}, bf16[512,256]{1,0:T(8,128)(2,1)S(1)}...) custom-call(s32[1]{0:T(128)} %bitcast.2.me_ref, s32[1]{0:T(128)S(6)} %copy.19.count_ref, ...), custom_call_target="tpu_custom_call" | custom-call | flops 10737418240 | bytes 8388608 | tf_op jit(solution)/shard_map/attn_fwd/pallas_call | solution.py:191
  63.8 9.6 %collective-permute-done.6.a2 = bf16[512,256]{1,0:T(8,128)(2,1)S(1)} collective-permute-done((bf16[512,256]{1,0:T(8,128)(2,1)S(1)}, bf16[512,256]{1,0:T(8,128)(2,1)S(1)}, u32[]{:S(2)}, u32[]{:S(2)}) %collective-permute-start.6) | collective-permute-done | bytes 262176 | tf_op jit(solution)/shard_map/ppermute | solution.py:51
  73.4 4.9 %collective-permute-done.7.a3 = bf16[512,256]{1,0:T(8,128)(2,1)S(1)} collective-permute-done((bf16[512,256]{1,0:T(8,128)(2,1)S(1)}, bf16[512,256]{1,0:T(8,128)(2,1)S(1)}, u32[]{:S(2)}, u32[]{:S(2)}) %collective-permute-start.7) | collective-permute-done | bytes 262176 | tf_op jit(solution)/shard_map/ppermute | solution.py:51
  84.1 11.9 %ffn.2 = (bf16[1024,704]{1,0:T(8,128)(2,1)S(1)}, bf16[1024,704]{1,0:T(8,128)(2,1)S(1)}, bf16[1024,704]{1,0:T(8,128)(2,1)S(1)}, bf16[512,1024]{1,0:T(8,128)(2,1)S...) custom-call(bf16[512,1024]{1,0:T(8,128)(2,1)S(1)} %get-tuple-element.172.na.c0, ...), custom_call_target="tpu_custom_call" | custom-call | flops 8858370048 | bytes 10616832 | tf_op jit(solution)/shard_map/ffn/pallas_call | solution.py:365
  101.5 5.5 %collective-permute-done.10.na.c2 = bf16[512,1024]{1,0:T(8,128)(2,1)S(1)} collective-permute-done((bf16[512,1024]{1,0:T(8,128)(2,1)S(1)}, bf16[512,1024]{1,0:T(8,128)(2,1)S(1)}, u32[]{:S(2)}, u32[]{:S(2)}) %collective-permute-start.10) | collective-permute-done | bytes 1048608 | tf_op jit(solution)/shard_map/ppermute | solution.py:51
  109.7 21.9 %ffn.3 = (bf16[1024,704]{1,0:T(8,128)(2,1)S(1)}, bf16[1024,704]{1,0:T(8,128)(2,1)S(1)}, bf16[1024,704]{1,0:T(8,128)(2,1)S(1)}, bf16[512,1024]{1,0:T(8,128)(2,1)S...) custom-call(bf16[512,1024]{1,0:T(8,128)(2,1)S(1)} %collective-permute-done.10.na.c2, ...), custom_call_target="tpu_custom_call" | custom-call | flops 8858370048 | bytes 10616832 | tf_op jit(solution)/shard_map/ffn/pallas_call | solution.py:365
  148.8 3.6 %wgrad_cols.3 = (bf16[4,704,128]{2,1,0:T(8,128)(2,1)S(1)}, bf16[4,704,128]{2,1,0:T(8,128)(2,1)S(1)}) custom-call(s32[1]{0:T(128)} %bitcast.5.dp_ref, bf16[1024,704]{1,0:T(8,128)(2,1)S(1)} %copy-done.67, bf16[1024,704]{1,0:T(8,128)(2,1)S(1)} %copy-done.73, bf16[512,1024]{1,0:T(8,128)(2,1)S(1)} %copy-done.26, bf16[512,1024]{1,0:T(8,128)(2,1)S(1)} %copy-done.51, ...), custom_call_target="tpu_custom_call" | custom-call | flops 2952790016 | bytes 8519680 | tf_op jit(solution)/shard_map/wgrad_cols/pallas_call | solution.py:492
  158.2 3.6 %wgrad_cols.5 = (bf16[4,704,128]{2,1,0:T(8,128)(2,1)S(1)}, bf16[4,704,128]{2,1,0:T(8,128)(2,1)S(1)}) custom-call(s32[1]{0:T(128)} %bitcast.5.dp_ref, bf16[1024,704]{1,0:T(8,128)(2,1)S(1)} %copy-done.63, bf16[1024,704]{1,0:T(8,128)(2,1)S(1)} %copy-done.69, bf16[512,1024]{1,0:T(8,128)(2,1)S(1)} %copy-done.47, bf16[512,1024]{1,0:T(8,128)(2,1)S(1)} %copy-done.49, ...), custom_call_target="tpu_custom_call" | custom-call | flops 2952790016 | bytes 8519680 | tf_op jit(solution)/shard_map/wgrad_cols/pallas_call | solution.py:492
  161.8 9.6 %collective-permute-done.20.b_ref = bf16[4,704,128]{2,1,0:T(8,128)(2,1)S(1)} collective-permute-done((bf16[4,704,128]{2,1,0:T(8,128)(2,1)S(1)}, bf16[4,704,128]{2,1,0:T(8,128)(2,1)S(1)}, u32[]{:S(2)}, u32[]{:S(2)}) %collective-permute-start.20) | collective-permute-done | bytes 720928 | tf_op jit(solution)/shard_map/ppermute | solution.py:51
  179.6 6.4 %collective-permute-done.24.b_ref = bf16[4,704,128]{2,1,0:T(8,128)(2,1)S(1)} collective-permute-done((bf16[4,704,128]{2,1,0:T(8,128)(2,1)S(1)}, bf16[4,704,128]{2,1,0:T(8,128)(2,1)S(1)}, u32[]{:S(2)}, u32[]{:S(2)}) %collective-permute-start.24) | collective-permute-done | bytes 720928 | tf_op jit(solution)/shard_map/ppermute | solution.py:51
  188.5 6.7 %collective-permute-done.22.d2_ref = bf16[512,256]{1,0:T(8,128)(2,1)S(1)} collective-permute-done((bf16[512,256]{1,0:T(8,128)(2,1)S(1)}, bf16[512,256]{1,0:T(8,128)(2,1)S(1)}, u32[]{:S(2)}, u32[]{:S(2)}) %collective-permute-start.22) | collective-permute-done | bytes 262176 | tf_op jit(solution)/shard_map/ppermute | solution.py:51
  201.5 16.6 %attn_bwd.2.g_ref.g0_ref = bf16[2048,384]{1,0:T(8,128)(2,1)S(1)} custom-call(s32[1]{0:T(128)} %bitcast.2.me_ref, s32[1]{0:T(128)S(6)} %copy.19.count_ref, bf16[2048,768]{1,0:T(8,128)(2,1)S(1)} %copy-done.75, bf16[2048,768]{1,0:T(8,128)(2,1)S(1)} %copy-done.75, bf16[2048,768]{1,0:T(8,128)(2,1)S(1)} %copy-done.75, ...), custom_call_target="tpu_custom_call" | custom-call | flops 10737418240 | bytes 4194304 | tf_op jit(solution)/shard_map/attn_bwd/pallas_call | solution.py:274
  227.1 4.1 %wgrad_qkv.2 = (bf16[4,128,640]{2,1,0:T(8,128)(2,1)S(1)}, bf16[4,128,640]{2,1,0:T(8,128)(2,1)S(1)}) custom-call(s32[1]{0:T(128)} %bitcast.2.me_ref, s32[1]{0:T(128)} %bitcast.5.dp_ref, bf16[2048,384]{1,0:T(8,128)(2,1)S(1)} %attn_bwd.2.g_ref.g0_ref, bf16[512,1024]{1,0:T(8,128)(2,1)S(1)} %copy-done.7, bf16[512,1024]{1,0:T(8,128)(2,1)S(1)} %copy-done.22, ...), custom_call_target="tpu_custom_call" | custom-call | flops 1610612736 | bytes 8650752 | tf_op jit(solution)/shard_map/wgrad_qkv/pallas_call | solution.py:554
  233.5 16.4 %attn_bwd.3.g1_ref.g_ref = bf16[2048,384]{1,0:T(8,128)(2,1)S(1)} custom-call(s32[1]{0:T(128)} %bitcast.2.me_ref, s32[1]{0:T(128)S(6)} %copy.19.count_ref, bf16[2048,768]{1,0:T(8,128)(2,1)S(1)} %copy-done.75, bf16[2048,768]{1,0:T(8,128)(2,1)S(1)} %copy-done.75, bf16[2048,768]{1,0:T(8,128)(2,1)S(1)} %copy-done.75, ...), custom_call_target="tpu_custom_call" | custom-call | flops 10737418240 | bytes 4194304 | tf_op jit(solution)/shard_map/attn_bwd/pallas_call | solution.py:274
  250.2 5.9 %collective-permute-done.32 = bf16[512,1024]{1,0:T(8,128)(2,1)S(1)} collective-permute-done((bf16[512,1024]{1,0:T(8,128)(2,1)S(1)}, bf16[512,1024]{1,0:T(8,128)(2,1)S(1)}, u32[]{:S(2)}, u32[]{:S(2)}) %collective-permute-start.32) | collective-permute-done | bytes 1048608 | tf_op jit(solution)/shard_map/ppermute | solution.py:51
  266.5 3.7 %wgrad_qkv.3 = (bf16[4,128,384]{2,1,0:T(8,128)(2,1)S(1)}, bf16[4,128,384]{2,1,0:T(8,128)(2,1)S(1)}) custom-call(s32[1]{0:T(128)} %bitcast.2.me_ref, s32[1]{0:T(128)} %bitcast.5.dp_ref, bf16[2048,384]{1,0:T(8,128)(2,1)S(1)} %attn_bwd.3.g1_ref.g_ref, bf16[512,1024]{1,0:T(8,128)(2,1)S(1)} %copy-done.7, bf16[512,1024]{1,0:T(8,128)(2,1)S(1)} %copy-done.22, ...), custom_call_target="tpu_custom_call" | custom-call | flops 1610612736 | bytes 6553600 | tf_op jit(solution)/shard_map/wgrad_qkv/pallas_call | solution.py:554
  278.3 5.3 %collective-permute-done.42 = bf16[2,128,640]{2,1,0:T(8,128)(2,1)S(1)} collective-permute-done((bf16[2,128,640]{2,1,0:T(8,128)(2,1)S(1)}, bf16[2,128,640]{2,1,0:T(8,128)(2,1)S(1)}, u32[]{:S(2)}, u32[]{:S(2)}) %collective-permute-start.42) | collective-permute-done | bytes 327712 | tf_op jit(solution)/shard_map/ppermute | solution.py:51
  288.9 12.7 %collective-permute-done.45 = bf16[2,128,640]{2,1,0:T(8,128)(2,1)S(1)} collective-permute-done((bf16[2,128,640]{2,1,0:T(8,128)(2,1)S(1)}, bf16[2,128,640]{2,1,0:T(8,128)(2,1)S(1)}, u32[]{:S(2)}, u32[]{:S(2)}) %collective-permute-start.45) | collective-permute-done | bytes 327712 | tf_op jit(solution)/shard_map/ppermute | solution.py:51
  307.9 7.8 %collective-permute-done.47 = bf16[2,128,640]{2,1,0:T(8,128)(2,1)S(1)} collective-permute-done((bf16[2,128,640]{2,1,0:T(8,128)(2,1)S(1)}, bf16[2,128,640]{2,1,0:T(8,128)(2,1)S(1)}, u32[]{:S(2)}, u32[]{:S(2)}) %collective-permute-start.47) | collective-permute-done | bytes 327712 | tf_op jit(solution)/shard_map/ppermute | solution.py:51
  315.9 4.9 %collective-permute-done.50.s_ref = bf16[4,704,128]{2,1,0:T(8,128)(2,1)S(1)} collective-permute-done((bf16[4,704,128]{2,1,0:T(8,128)(2,1)S(1)}, bf16[4,704,128]{2,1,0:T(8,128)(2,1)S(1)}, u32[]{:S(2)}, u32[]{:S(2)}) %collective-permute-start.50) | collective-permute-done | bytes 720928 | tf_op jit(solution)/shard_map/ppermute | solution.py:51
  323.3 4.4 %collective-permute-done.55 = bf16[2,704,128]{2,1,0:T(8,128)(2,1)S(1)} collective-permute-done((bf16[2,704,128]{2,1,0:T(8,128)(2,1)S(1)}, bf16[2,704,128]{2,1,0:T(8,128)(2,1)S(1)}, u32[]{:S(2)}, u32[]{:S(2)}) %collective-permute-start.55) | collective-permute-done | bytes 360480 | tf_op jit(solution)/shard_map/ppermute | solution.py:51
  337.7 7.4 %collective-permute-done.56.s_ref = bf16[4,704,128]{2,1,0:T(8,128)(2,1)S(1)} collective-permute-done((bf16[4,704,128]{2,1,0:T(8,128)(2,1)S(1)}, bf16[4,704,128]{2,1,0:T(8,128)(2,1)S(1)}, u32[]{:S(2)}, u32[]{:S(2)}) %collective-permute-start.56) | collective-permute-done | bytes 720928 | tf_op jit(solution)/shard_map/ppermute | solution.py:51
  348.6 4.7 %collective-permute-done.54 = f32[1,1024]{1,0:T(1,128)S(1)} collective-permute-done((f32[1,1024]{1,0:T(1,128)S(1)}, f32[1,1024]{1,0:T(1,128)S(1)}, u32[]{:S(2)}, u32[]{:S(2)}) %collective-permute-start.54) | collective-permute-done | bytes 4128 | tf_op jit(solution)/shard_map/ppermute | solution.py:51
  (311 shorter events, 134.8 us)
Async XLA Ops:
  3.5 26.3 %collective-permute-start = (bf16[512,1024]{1,0:T(8,128)(2,1)S(1)}, bf16[512,1024]{1,0:T(8,128)(2,1)S(1)}, u32[]{:S(2)}, u32[]{:S(2)}) collective-permute-start(bf16[512,1024]{1,0:T(8,128)(2,1)S(1)} %norm.1.a_ref.n0), channel_id=1, source_target_pairs={{0,2},{1,3},{2,0},{3,1},{4,6},{5,7},{6,4},{7,5},{8,10},{9,11},{10,... | collective-permute-start | bytes 3145736 | tf_op jit(solution)/shard_map/ppermute | solution.py:51
  30.5 30.9 %collective-permute-start.4 = (bf16[256,1024]{1,0:T(8,128)(2,1)S(1)}, bf16[256,1024]{1,0:T(8,128)(2,1)S(1)}, u32[]{:S(2)}, u32[]{:S(2)}) collective-permute-start(bf16[256,1024]{1,0:T(8,128)(2,1)S(1)} %copy-done.8), channel_id=1, source_target_pairs={{0,2},{1,3},{2,0},{3,1},{4,6},{5,7},{6,4},{7,5},{8,10},{9,11},{10,... | collective-permute-start | bytes 1572872 | tf_op jit(solution)/shard_map/ppermute | solution.py:51
  32.6 45.6 %collective-permute-start.3 = (bf16[512,1024]{1,0:T(8,128)(2,1)}, bf16[512,1024]{1,0:T(8,128)(2,1)S(1)}, u32[]{:S(2)}, u32[]{:S(2)}) collective-permute-start(bf16[512,1024]{1,0:T(8,128)(2,1)} %cot.1), channel_id=1, source_target_pairs={{0,2},{1,3},{2,0},{3,1},{4,6},{5,7},{6,4},{7,5},{8,10},{9,11},{10,... | collective-permute-start | bytes 3145736 | tf_op jit(solution)/shard_map/ppermute | solution.py:51
  81.7 25.4 %collective-permute-start.10 = (bf16[512,1024]{1,0:T(8,128)(2,1)S(1)}, bf16[512,1024]{1,0:T(8,128)(2,1)S(1)}, u32[]{:S(2)}, u32[]{:S(2)}) collective-permute-start(bf16[512,1024]{1,0:T(8,128)(2,1)S(1)} %get-tuple-element.172.na.c0), channel_id=1, source_target_pairs={{0,2},{1,3},{2,0},{3,1},{4,6},{5,7},{6,4},{7,5},{8,10},{9,11},{10,... | collective-permute-start | bytes 3145736 | tf_op jit(solution)/shard_map/ppermute | solution.py:51
  83.4 24.2 %collective-permute-start.16 = (bf16[512,1024]{1,0:T(8,128)(2,1)S(1)}, bf16[512,1024]{1,0:T(8,128)(2,1)S(1)}, u32[]{:S(2)}, u32[]{:S(2)}) collective-permute-start(bf16[512,1024]{1,0:T(8,128)(2,1)S(1)} %collective-permute-done.3.ca.c2), channel_id=1, source_target_pairs={{0,1},{1,0},{2,3},{3,2},{4,5},{5,4},{6,7},{7,6},{8,9},{9,8},{10,11... | collective-permute-start | bytes 3145736 | tf_op jit(solution)/shard_map/ppermute | solution.py:51
  107.1 27.9 %collective-permute-start.13 = (bf16[512,1024]{1,0:T(8,128)(2,1)S(1)}, bf16[512,1024]{1,0:T(8,128)(2,1)S(1)}, u32[]{:S(2)}, u32[]{:S(2)}) collective-permute-start(bf16[512,1024]{1,0:T(8,128)(2,1)S(1)} %get-tuple-element.181), channel_id=1, source_target_pairs={{0,1},{1,0},{2,3},{3,2},{4,5},{5,4},{6,7},{7,6},{8,9},{9,8},{10,11... | collective-permute-start | bytes 3145736 | tf_op jit(solution)/shard_map/ppermute | solution.py:51
  107.6 27.4 %collective-permute-start.14 = (bf16[512,1024]{1,0:T(8,128)(2,1)S(1)}, bf16[512,1024]{1,0:T(8,128)(2,1)S(1)}, u32[]{:S(2)}, u32[]{:S(2)}) collective-permute-start(bf16[512,1024]{1,0:T(8,128)(2,1)S(1)} %get-tuple-element.182), channel_id=1, source_target_pairs={{0,1},{1,0},{2,3},{3,2},{4,5},{5,4},{6,7},{7,6},{8,9},{9,8},{10,11... | collective-permute-start | bytes 3145736 | tf_op jit(solution)/shard_map/ppermute | solution.py:51
  139.1 34.2 %collective-permute-start.18 = (bf16[512,1024]{1,0:T(8,128)(2,1)}, bf16[512,1024]{1,0:T(8,128)(2,1)}, u32[]{:S(2)}, u32[]{:S(2)}) collective-permute-start(bf16[512,1024]{1,0:T(8,128)(2,1)} %get-tuple-element.192), channel_id=1, source_target_pairs={{0,1},{1,0},{2,3},{3,2},{4,5},{5,4},{6,7},{7,6},{8,9},{9,8},{10,11... | collective-permute-start | bytes 3145736 | tf_op jit(solution)/shard_map/ppermute | solution.py:51
  139.3 35.6 %collective-permute-start.19 = (bf16[512,1024]{1,0:T(8,128)(2,1)}, bf16[512,1024]{1,0:T(8,128)(2,1)S(1)}, u32[]{:S(2)}, u32[]{:S(2)}) collective-permute-start(bf16[512,1024]{1,0:T(8,128)(2,1)} %add_convert_fusion.2), channel_id=1, source_target_pairs={{0,2},{1,3},{2,0},{3,1},{4,6},{5,7},{6,4},{7,5},{8,10},{9,11},{10,... | collective-permute-start | bytes 3145736 | tf_op jit(solution)/shard_map/ppermute | solution.py:51
  157.6 28.4 %collective-permute-start.24 = (bf16[4,704,128]{2,1,0:T(8,128)(2,1)S(1)}, bf16[4,704,128]{2,1,0:T(8,128)(2,1)S(1)}, u32[]{:S(2)}, u32[]{:S(2)}) collective-permute-start(bf16[4,704,128]{2,1,0:T(8,128)(2,1)S(1)} %get-tuple-element.216), channel_id=1, source_target_pairs={{0,4},{4,0},{8,12},{12,8},{16,20},{20,16},{24,28},{28,24},{1,5},{5... | collective-permute-start | bytes 2162696 | tf_op jit(solution)/shard_map/ppermute | solution.py:51
  186.9 38.4 %collective-permute-start.30 = (bf16[4,704,128]{2,1,0:T(8,128)(2,1)S(1)}, bf16[4,704,128]{2,1,0:T(8,128)(2,1)S(1)}, u32[]{:S(2)}, u32[]{:S(2)}) collective-permute-start(bf16[4,704,128]{2,1,0:T(8,128)(2,1)S(1)} %get-tuple-element.237), channel_id=1, source_target_pairs={{0,8},{4,12},{8,0},{12,4},{16,24},{20,28},{24,16},{28,20},{1,9},{5... | collective-permute-start | bytes 2162696 | tf_op jit(solution)/shard_map/ppermute | solution.py:51
  195.2 25.6 %collective-permute-start.29 = (bf16[2,704,128]{2,1,0:T(8,128)(2,1)S(1)}, bf16[2,704,128]{2,1,0:T(8,128)(2,1)S(1)}, u32[]{:S(2)}, u32[]{:S(2)}) collective-permute-start(bf16[2,704,128]{2,1,0:T(8,128)(2,1)S(1)} %get-tuple-element.220), channel_id=1, source_target_pairs={{0,8},{4,12},{8,0},{12,4},{16,24},{20,28},{24,16},{28,20},{1,9},{5... | collective-permute-start | bytes 1081352 | tf_op jit(solution)/shard_map/ppermute | solution.py:51
  197.3 23.6 %collective-permute-start.28 = (bf16[2,704,128]{2,1,0:T(8,128)(2,1)S(1)}, bf16[2,704,128]{2,1,0:T(8,128)(2,1)S(1)}, u32[]{:S(2)}, u32[]{:S(2)}) collective-permute-start(bf16[2,704,128]{2,1,0:T(8,128)(2,1)S(1)} %add_convert_fusion.9), channel_id=1, source_target_pairs={{0,16},{4,20},{8,24},{12,28},{16,0},{20,4},{24,8},{28,12},{1,17},{... | collective-permute-start | bytes 1081352 | tf_op jit(solution)/shard_map/ppermute | solution.py:51
  200.1 27.0 %collective-permute-start.31 = (bf16[256,1024]{1,0:T(8,128)(2,1)S(1)}, bf16[256,1024]{1,0:T(8,128)(2,1)S(1)}, u32[]{:S(2)}, u32[]{:S(2)}) collective-permute-start(bf16[256,1024]{1,0:T(8,128)(2,1)S(1)} %add_convert_fusion.3.rest_0_), channel_id=1, source_target_pairs={{0,2},{1,3},{2,0},{3,1},{4,6},{5,7},{6,4},{7,5},{8,10},{9,11},{10,... | collective-permute-start | bytes 1572872 | tf_op jit(solution)/shard_map/ppermute | solution.py:51
  221.1 28.8 %collective-permute-start.35 = (bf16[2,704,128]{2,1,0:T(8,128)(2,1)S(1)}, bf16[2,704,128]{2,1,0:T(8,128)(2,1)S(1)}, u32[]{:S(2)}, u32[]{:S(2)}) collective-permute-start(bf16[2,704,128]{2,1,0:T(8,128)(2,1)S(1)} %get-tuple-element.294), channel_id=1, source_target_pairs={{0,16},{4,20},{8,24},{12,28},{16,0},{20,4},{24,8},{28,12},{1,17},{... | collective-permute-start | bytes 1081352 | tf_op jit(solution)/shard_map/ppermute | solution.py:51
  223.6 26.2 %collective-permute-start.34 = (bf16[2,704,128]{2,1,0:T(8,128)(2,1)S(1)}, bf16[2,704,128]{2,1,0:T(8,128)(2,1)S(1)}, u32[]{:S(2)}, u32[]{:S(2)}) collective-permute-start(bf16[2,704,128]{2,1,0:T(8,128)(2,1)S(1)} %get-tuple-element.295), channel_id=1, source_target_pairs={{0,8},{4,12},{8,0},{12,4},{16,24},{20,28},{24,16},{28,20},{1,9},{5... | collective-permute-start | bytes 1081352 | tf_op jit(solution)/shard_map/ppermute | solution.py:51
  225.5 24.6 %collective-permute-start.36 = (bf16[2,704,128]{2,1,0:T(8,128)(2,1)S(1)}, bf16[2,704,128]{2,1,0:T(8,128)(2,1)S(1)}, u32[]{:S(2)}, u32[]{:S(2)}) collective-permute-start(bf16[2,704,128]{2,1,0:T(8,128)(2,1)S(1)} %get-tuple-element.239), channel_id=1, source_target_pairs={{0,4},{4,0},{8,12},{12,8},{16,20},{20,16},{24,28},{28,24},{1,5},{5... | collective-permute-start | bytes 1081352 | tf_op jit(solution)/shard_map/ppermute | solution.py:51
  231.8 24.3 %collective-permute-start.32 = (bf16[512,1024]{1,0:T(8,128)(2,1)S(1)}, bf16[512,1024]{1,0:T(8,128)(2,1)S(1)}, u32[]{:S(2)}, u32[]{:S(2)}) collective-permute-start(bf16[512,1024]{1,0:T(8,128)(2,1)S(1)} %add_convert_fusion.1), channel_id=1, source_target_pairs={{0,2},{1,3},{2,0},{3,1},{4,6},{5,7},{6,4},{7,5},{8,10},{9,11},{10,... | collective-permute-start | bytes 3145736 | tf_op jit(solution)/shard_map/ppermute | solution.py:51
  258.4 28.5 %collective-permute-start.46 = (bf16[4,704,128]{2,1,0:T(8,128)(2,1)S(1)}, bf16[4,704,128]{2,1,0:T(8,128)(2,1)S(1)}, u32[]{:S(2)}, u32[]{:S(2)}) collective-permute-start(bf16[4,704,128]{2,1,0:T(8,128)(2,1)S(1)} %pad_maximum_fusion.k_ref), channel_id=1, source_target_pairs={{0,4},{4,0},{8,12},{12,8},{16,20},{20,16},{24,28},{28,24},{1,5},{5... | collective-permute-start | bytes 2162696 | tf_op jit(solution)/shard_map/ppermute | solution.py:51
  259.9 23.7 %collective-permute-start.41 = (bf16[2,704,128]{2,1,0:T(8,128)(2,1)S(1)}, bf16[2,704,128]{2,1,0:T(8,128)(2,1)S(1)}, u32[]{:S(2)}, u32[]{:S(2)}) collective-permute-start(bf16[2,704,128]{2,1,0:T(8,128)(2,1)S(1)} %add_convert_fusion.5), channel_id=1, source_target_pairs={{0,16},{4,20},{8,24},{12,28},{16,0},{20,4},{24,8},{28,12},{1,17},{... | collective-permute-start | bytes 1081352 | tf_op jit(solution)/shard_map/ppermute | solution.py:51
  265.5 40.3 %collective-permute-start.39 = (bf16[512,1024]{1,0:T(8,128)(2,1)S(1)}, bf16[512,1024]{1,0:T(8,128)(2,1)S(1)}, u32[]{:S(2)}, u32[]{:S(2)}) collective-permute-start(bf16[512,1024]{1,0:T(8,128)(2,1)S(1)} %add_convert_fusion), channel_id=1, source_target_pairs={{0,2},{1,3},{2,0},{3,1},{4,6},{5,7},{6,4},{7,5},{8,10},{9,11},{10,... | collective-permute-start | bytes 3145736 | tf_op jit(solution)/shard_map/ppermute | solution.py:51
  305.2 22.5 %collective-permute-start.55 = (bf16[2,704,128]{2,1,0:T(8,128)(2,1)S(1)}, bf16[2,704,128]{2,1,0:T(8,128)(2,1)S(1)}, u32[]{:S(2)}, u32[]{:S(2)}) collective-permute-start(bf16[2,704,128]{2,1,0:T(8,128)(2,1)S(1)} %add_convert_fusion.4), channel_id=1, source_target_pairs={{0,4},{4,0},{8,12},{12,8},{16,20},{20,16},{24,28},{28,24},{1,5},{5... | collective-permute-start | bytes 1081352 | tf_op jit(solution)/shard_map/ppermute | solution.py:51
  329.5 24.4 %collective-permute-start.60 = (bf16[4,128,640]{2,1,0:T(8,128)(2,1)S(1)}, bf16[4,128,640]{2,1,0:T(8,128)(2,1)S(1)}, u32[]{:S(2)}, u32[]{:S(2)}) collective-permute-start(bf16[4,128,640]{2,1,0:T(8,128)(2,1)S(1)} %pad_maximum_fusion.3.a_ref.ak), channel_id=1, source_target_pairs={{0,4},{4,0},{8,12},{12,8},{16,20},{20,16},{24,28},{28,24},{1,5},{5... | collective-permute-start | bytes 1966088 | tf_op jit(solution)/shard_map/ppermute | solution.py:51
  331.0 22.9 %collective-permute-start.61 = (bf16[4,128,384]{2,1,0:T(8,128)(2,1)S(1)}, bf16[4,128,384]{2,1,0:T(8,128)(2,1)S(1)}, u32[]{:S(2)}, u32[]{:S(2)}) collective-permute-start(bf16[4,128,384]{2,1,0:T(8,128)(2,1)S(1)} %pad_maximum_fusion.4.b_ref.bk), channel_id=1, source_target_pairs={{0,4},{4,0},{8,12},{12,8},{16,20},{20,16},{24,28},{28,24},{1,5},{5... | collective-permute-start | bytes 1179656 | tf_op jit(solution)/shard_map/ppermute | solution.py:51
  (118 other events, 1176.9 us)
where the time goes:
time: 361 us; the launch traced here: 357 us
  waiting for transfers between devices  133 us (37%)
  Pallas kernels  131 us (36%)
  starting transfers between devices  55.2 us (15%)
  local copies, waits for them, and re-layouts  26.6 us (7%)
  other arithmetic  8.1 us (2%)
    ppermute x62, waiting for transfers between devices, swap(): return lax.ppermute(value, axis, [(i, i ^ bit) for i in range(size)])  133 us
    ppermute x62, starting transfers between devices, swap(): return lax.ppermute(value, axis, [(i, i ^ bit) for i in range(size)])  55.2 us
    pallas_call x2, Pallas kernels, ffn(): pl.pallas_call(functools.partial(ffn_kernel, half=half), grid=(2 * half,)...  33.8 us
    pallas_call x2, Pallas kernels, attn_bwd(): pl.pallas_call(functools.partial(attn_bwd_kernel, length=length, block=bl...  33 us
    unnamed x160, local copies, waits for them, and re-layouts  26.6 us
    pallas_call x1, Pallas kernels, attn_fwd(): pl.pallas_call(functools.partial(attn_fwd_kernel, length=length, columns=...  22.1 us
    pallas_call x3, Pallas kernels, wgrad_cols(): pl.pallas_call(functools.partial(wgrad_cols_kernel, each=each, lead=lead)...  10.8 us
    pallas_call x2, Pallas kernels, wgrad_qkv(): pl.pallas_call(functools.partial(wgrad_qkv_kernel, each=each), in_specs=[...  7.8 us
  transfers between devices with their start and end apart: 62, of which 27 were waited for; matrix products, arithmetic and copies ran while one was open for 2% of the time, Pallas kernels for 36%

commit v1 on v0

--- a/solution.py
+++ b/solution.py
@@ -203,7 +203,7 @@
 
 
 def attn_bwd_kernel(me_ref, count_ref, q_ref, k_ref, v_ref, d0_ref, d1_ref, d2_ref, d3_ref, o_ref, lse_ref, *rest, length, block, pair):
-    g_ref, do_all, kaug, qaug, dom, dq = rest[-6:]
+    g_ref, do_all, kaug, qaug, dom, vaug, dq = rest[-7:]
     parity = pl.program_id(0)
     rows_each = length // 4
     me = me_ref[0]
@@ -218,16 +218,24 @@
     sel, spare = head_lanes(length, parity)
     row = lax.broadcasted_iota(jnp.int32, (length, LANES), 0)
     bias = jnp.where(row < count_ref[0], 0.0, -1e30)
-    kaug[...] = jnp.where(sel, k_ref[...].astype(f32), jnp.where(spare, bias, 0.0)).astype(bf16)
-    qaug[...] = jnp.where(sel, q_ref[...].astype(f32), jnp.where(spare, 1.0, 0.0)).astype(bf16)
+    offset = lax.broadcasted_iota(jnp.int32, (length, LANES), 1) - (1 - parity) * HD
+    extra = (offset >= 1) & (offset <= 3)
+
+    def in_lanes(column):
+        high = column.astype(bf16).astype(f32)
+        rest_1 = column - high
+        middle = rest_1.astype(bf16).astype(f32)
+        return jnp.where(offset == 1, high, jnp.where(offset == 2, middle, jnp.where(offset == 3, rest_1 - middle, 0.0)))
+
+    ones = jnp.where(extra, 1.0, 0.0)
+    kaug[...] = jnp.where(sel, k_ref[...].astype(f32), jnp.where(spare, bias, ones)).astype(bf16)
+    vaug[...] = jnp.where(sel, v_ref[...].astype(f32), ones).astype(bf16)
+    lse = lse_ref[pl.ds(2 * pair + parity, 1), :]
+    shift = in_lanes(jnp.transpose(jnp.broadcast_to(lse * (-1.0 / c), (LANES, length))))
+    qaug[...] = jnp.where(sel, q_ref[...].astype(f32), jnp.where(spare, 1.0, shift)).astype(bf16)
     do = jnp.where(sel, do_all[...].astype(f32), 0.0)
-    dom[...] = do.astype(bf16)
-    prod = do * o_ref[...].astype(f32)
-    hi = prod.astype(bf16)
-    lo = (prod - hi.astype(f32)).astype(bf16)
-    ones = jnp.ones((8, LANES), bf16)
-    delta = (dot(ones, hi, NT) + dot(ones, lo, NT))[0:1]
-    lse = lse_ref[pl.ds(2 * pair + parity, 1), :]
+    delta = jnp.sum(do * o_ref[...].astype(f32), axis=1, keepdims=True)
+    dom[...] = (do + in_lanes(jnp.broadcast_to(-delta, (length, LANES)))).astype(bf16)
     sel_b, _ = head_lanes(block, parity)
     ki = lax.broadcasted_iota(jnp.int32, (block, block), 0)
     qi = lax.broadcasted_iota(jnp.int32, (block, block), 1)
@@ -236,15 +244,15 @@
         first = j * block
         last = first + block
         kj = kaug[first:last]
-        vj = v_ref[first:last]
+        vj = vaug[first:last]
 
         def part(a, b, diag):
             s = dot(kj, qaug[a:b], NT)
             if diag:
                 s = jnp.where(ki <= qi, s, -1e30)
-            p = jnp.exp2(s * c - lse[:, a:b])
+            p = jnp.exp2(s * c)
             dp = dot(vj, dom[a:b], NT)
-            ds = (p * (dp - delta[:, a:b])).astype(bf16)
+            ds = (p * dp).astype(bf16)
             dv = dot(p.astype(bf16), dom[a:b])
             dk = dot(ds, qaug[a:b])
             dq[a:b] += dot(ds, kj, TN)
@@ -281,7 +289,7 @@
         + [part(length, pair), whole(heads, length)]
         + [pl.BlockSpec(memory_space=pl.ANY)] * len(deps),
         out_specs=whole(length, 3 * LANES),
-        scratch_shapes=[pltpu.VMEM((length, LANES), bf16)] * 4 + [pltpu.VMEM((length, LANES), f32)],
+        scratch_shapes=[pltpu.VMEM((length, LANES), bf16)] * 5 + [pltpu.VMEM((length, LANES), f32)],
         compiler_params=params(),
         cost_estimate=cost(20 * length * length * LANES, 2 * length * LANES * 8, length * length),
         name="attn_bwd",

time: 361 us -> 361 us (level)
  no operation moved by 1% of the time
where the time goes in v1:
time: 361 us; the launch traced here: 357 us
  Pallas kernels  132 us (37%)
  waiting for transfers between devices  132 us (37%)
  starting transfers between devices  55.2 us (15%)
  local copies, waits for them, and re-layouts  26.6 us (7%)
  other arithmetic  8.1 us (2%)
    ppermute x62, waiting for transfers between devices, swap(): return lax.ppermute(value, axis, [(i, i ^ bit) for i in range(size)])  132 us
    ppermute x62, starting transfers between devices, swap(): return lax.ppermute(value, axis, [(i, i ^ bit) for i in range(size)])  55.2 us
    pallas_call x2, Pallas kernels, attn_bwd(): pl.pallas_call(functools.partial(attn_bwd_kernel, length=length, block=bl...  34.1 us
    pallas_call x2, Pallas kernels, ffn(): pl.pallas_call(functools.partial(ffn_kernel, half=half), grid=(2 * half,)...  33.8 us
    unnamed x160, local copies, waits for them, and re-layouts  26.6 us
    pallas_call x1, Pallas kernels, attn_fwd(): pl.pallas_call(functools.partial(attn_fwd_kernel, length=length, columns=...  22.1 us
    pallas_call x3, Pallas kernels, wgrad_cols(): pl.pallas_call(functools.partial(wgrad_cols_kernel, each=each, lead=lead)...  10.8 us
    pallas_call x2, Pallas kernels, wgrad_qkv(): pl.pallas_call(functools.partial(wgrad_qkv_kernel, each=each), in_specs=[...  7.8 us
  transfers between devices with their start and end apart: 62, of which 27 were waited for; matrix products, arithmetic and copies ran while one was open for 2% of the time, Pallas kernels for 36%

profile of v1, /device:TPU:0, one launch (start us, length us, event | category | flops | bytes accessed | tf_op | source)
XLA Modules:
  0.0 357.0 jit_solution(14619677165978767263)
XLA Ops:
  9.9 20.0 %collective-permute-done.n2_ref.n2 = bf16[512,1024]{1,0:T(8,128)(2,1)S(1)} collective-permute-done((bf16[512,1024]{1,0:T(8,128)(2,1)S(1)}, bf16[512,1024]{1,0:T(8,128)(2,1)S(1)}, u32[]{:S(2)}, u32[]{:S(2)}) %collective-permute-start) | collective-permute-done | bytes 1048608 | tf_op jit(solution)/shard_map/ppermute | solution.py:51
  36.7 22.1 %attn_fwd.1 = (bf16[2048,768]{1,0:T(8,128)(2,1)S(1)}, bf16[2048,256]{1,0:T(8,128)(2,1)S(1)}, f32[4,2048]{1,0:T(4,128)S(1)}, bf16[512,256]{1,0:T(8,128)(2,1)S(1)}...) custom-call(s32[1]{0:T(128)} %bitcast.2.me_ref, s32[1]{0:T(128)S(6)} %copy.19.count_ref, ...), custom_call_target="tpu_custom_call" | custom-call | flops 10737418240 | bytes 8388608 | tf_op jit(solution)/shard_map/attn_fwd/pallas_call | solution.py:191
  63.8 9.6 %collective-permute-done.6.a2 = bf16[512,256]{1,0:T(8,128)(2,1)S(1)} collective-permute-done((bf16[512,256]{1,0:T(8,128)(2,1)S(1)}, bf16[512,256]{1,0:T(8,128)(2,1)S(1)}, u32[]{:S(2)}, u32[]{:S(2)}) %collective-permute-start.6) | collective-permute-done | bytes 262176 | tf_op jit(solution)/shard_map/ppermute | solution.py:51
  73.4 4.9 %collective-permute-done.7.a3 = bf16[512,256]{1,0:T(8,128)(2,1)S(1)} collective-permute-done((bf16[512,256]{1,0:T(8,128)(2,1)S(1)}, bf16[512,256]{1,0:T(8,128)(2,1)S(1)}, u32[]{:S(2)}, u32[]{:S(2)}) %collective-permute-start.7) | collective-permute-done | bytes 262176 | tf_op jit(solution)/shard_map/ppermute | solution.py:51
  84.1 11.9 %ffn.2 = (bf16[1024,704]{1,0:T(8,128)(2,1)S(1)}, bf16[1024,704]{1,0:T(8,128)(2,1)S(1)}, bf16[1024,704]{1,0:T(8,128)(2,1)S(1)}, bf16[512,1024]{1,0:T(8,128)(2,1)S...) custom-call(bf16[512,1024]{1,0:T(8,128)(2,1)S(1)} %get-tuple-element.172.na.c0, ...), custom_call_target="tpu_custom_call" | custom-call | flops 8858370048 | bytes 10616832 | tf_op jit(solution)/shard_map/ffn/pallas_call | solution.py:373
  101.5 5.5 %collective-permute-done.10.na.c2 = bf16[512,1024]{1,0:T(8,128)(2,1)S(1)} collective-permute-done((bf16[512,1024]{1,0:T(8,128)(2,1)S(1)}, bf16[512,1024]{1,0:T(8,128)(2,1)S(1)}, u32[]{:S(2)}, u32[]{:S(2)}) %collective-permute-start.10) | collective-permute-done | bytes 1048608 | tf_op jit(solution)/shard_map/ppermute | solution.py:51
  109.7 21.9 %ffn.3 = (bf16[1024,704]{1,0:T(8,128)(2,1)S(1)}, bf16[1024,704]{1,0:T(8,128)(2,1)S(1)}, bf16[1024,704]{1,0:T(8,128)(2,1)S(1)}, bf16[512,1024]{1,0:T(8,128)(2,1)S...) custom-call(bf16[512,1024]{1,0:T(8,128)(2,1)S(1)} %collective-permute-done.10.na.c2, ...), custom_call_target="tpu_custom_call" | custom-call | flops 8858370048 | bytes 10616832 | tf_op jit(solution)/shard_map/ffn/pallas_call | solution.py:373
  148.8 3.6 %wgrad_cols.3 = (bf16[4,704,128]{2,1,0:T(8,128)(2,1)S(1)}, bf16[4,704,128]{2,1,0:T(8,128)(2,1)S(1)}) custom-call(s32[1]{0:T(128)} %bitcast.5.dp_ref, bf16[1024,704]{1,0:T(8,128)(2,1)S(1)} %copy-done.67, bf16[1024,704]{1,0:T(8,128)(2,1)S(1)} %copy-done.73, bf16[512,1024]{1,0:T(8,128)(2,1)S(1)} %copy-done.26, bf16[512,1024]{1,0:T(8,128)(2,1)S(1)} %copy-done.51, ...), custom_call_target="tpu_custom_call" | custom-call | flops 2952790016 | bytes 8519680 | tf_op jit(solution)/shard_map/wgrad_cols/pallas_call | solution.py:500
  158.2 3.6 %wgrad_cols.5 = (bf16[4,704,128]{2,1,0:T(8,128)(2,1)S(1)}, bf16[4,704,128]{2,1,0:T(8,128)(2,1)S(1)}) custom-call(s32[1]{0:T(128)} %bitcast.5.dp_ref, bf16[1024,704]{1,0:T(8,128)(2,1)S(1)} %copy-done.63, bf16[1024,704]{1,0:T(8,128)(2,1)S(1)} %copy-done.69, bf16[512,1024]{1,0:T(8,128)(2,1)S(1)} %copy-done.47, bf16[512,1024]{1,0:T(8,128)(2,1)S(1)} %copy-done.49, ...), custom_call_target="tpu_custom_call" | custom-call | flops 2952790016 | bytes 8519680 | tf_op jit(solution)/shard_map/wgrad_cols/pallas_call | solution.py:500
  161.8 9.6 %collective-permute-done.20.b_ref = bf16[4,704,128]{2,1,0:T(8,128)(2,1)S(1)} collective-permute-done((bf16[4,704,128]{2,1,0:T(8,128)(2,1)S(1)}, bf16[4,704,128]{2,1,0:T(8,128)(2,1)S(1)}, u32[]{:S(2)}, u32[]{:S(2)}) %collective-permute-start.20) | collective-permute-done | bytes 720928 | tf_op jit(solution)/shard_map/ppermute | solution.py:51
  179.6 6.4 %collective-permute-done.24.b_ref = bf16[4,704,128]{2,1,0:T(8,128)(2,1)S(1)} collective-permute-done((bf16[4,704,128]{2,1,0:T(8,128)(2,1)S(1)}, bf16[4,704,128]{2,1,0:T(8,128)(2,1)S(1)}, u32[]{:S(2)}, u32[]{:S(2)}) %collective-permute-start.24) | collective-permute-done | bytes 720928 | tf_op jit(solution)/shard_map/ppermute | solution.py:51
  188.5 6.7 %collective-permute-done.22.d2_ref = bf16[512,256]{1,0:T(8,128)(2,1)S(1)} collective-permute-done((bf16[512,256]{1,0:T(8,128)(2,1)S(1)}, bf16[512,256]{1,0:T(8,128)(2,1)S(1)}, u32[]{:S(2)}, u32[]{:S(2)}) %collective-permute-start.22) | collective-permute-done | bytes 262176 | tf_op jit(solution)/shard_map/ppermute | solution.py:51
  201.5 17.2 %attn_bwd.2.g_ref.g0_ref = bf16[2048,384]{1,0:T(8,128)(2,1)S(1)} custom-call(s32[1]{0:T(128)} %bitcast.2.me_ref, s32[1]{0:T(128)S(6)} %copy.19.count_ref, bf16[2048,768]{1,0:T(8,128)(2,1)S(1)} %copy-done.75, bf16[2048,768]{1,0:T(8,128)(2,1)S(1)} %copy-done.75, bf16[2048,768]{1,0:T(8,128)(2,1)S(1)} %copy-done.75, ...), custom_call_target="tpu_custom_call" | custom-call | flops 10737418240 | bytes 4194304 | tf_op jit(solution)/shard_map/attn_bwd/pallas_call | solution.py:282
  227.1 4.1 %wgrad_qkv.2 = (bf16[4,128,640]{2,1,0:T(8,128)(2,1)S(1)}, bf16[4,128,640]{2,1,0:T(8,128)(2,1)S(1)}) custom-call(s32[1]{0:T(128)} %bitcast.2.me_ref, s32[1]{0:T(128)} %bitcast.5.dp_ref, bf16[2048,384]{1,0:T(8,128)(2,1)S(1)} %attn_bwd.2.g_ref.g0_ref, bf16[512,1024]{1,0:T(8,128)(2,1)S(1)} %copy-done.7, bf16[512,1024]{1,0:T(8,128)(2,1)S(1)} %copy-done.22, ...), custom_call_target="tpu_custom_call" | custom-call | flops 1610612736 | bytes 8650752 | tf_op jit(solution)/shard_map/wgrad_qkv/pallas_call | solution.py:562
  233.5 16.9 %attn_bwd.3.g1_ref.g_ref = bf16[2048,384]{1,0:T(8,128)(2,1)S(1)} custom-call(s32[1]{0:T(128)} %bitcast.2.me_ref, s32[1]{0:T(128)S(6)} %copy.19.count_ref, bf16[2048,768]{1,0:T(8,128)(2,1)S(1)} %copy-done.75, bf16[2048,768]{1,0:T(8,128)(2,1)S(1)} %copy-done.75, bf16[2048,768]{1,0:T(8,128)(2,1)S(1)} %copy-done.75, ...), custom_call_target="tpu_custom_call" | custom-call | flops 10737418240 | bytes 4194304 | tf_op jit(solution)/shard_map/attn_bwd/pallas_call | solution.py:282
  250.7 5.4 %collective-permute-done.32 = bf16[512,1024]{1,0:T(8,128)(2,1)S(1)} collective-permute-done((bf16[512,1024]{1,0:T(8,128)(2,1)S(1)}, bf16[512,1024]{1,0:T(8,128)(2,1)S(1)}, u32[]{:S(2)}, u32[]{:S(2)}) %collective-permute-start.32) | collective-permute-done | bytes 1048608 | tf_op jit(solution)/shard_map/ppermute | solution.py:51
  266.5 3.7 %wgrad_qkv.3 = (bf16[4,128,384]{2,1,0:T(8,128)(2,1)S(1)}, bf16[4,128,384]{2,1,0:T(8,128)(2,1)S(1)}) custom-call(s32[1]{0:T(128)} %bitcast.2.me_ref, s32[1]{0:T(128)} %bitcast.5.dp_ref, bf16[2048,384]{1,0:T(8,128)(2,1)S(1)} %attn_bwd.3.g1_ref.g_ref, bf16[512,1024]{1,0:T(8,128)(2,1)S(1)} %copy-done.7, bf16[512,1024]{1,0:T(8,128)(2,1)S(1)} %copy-done.22, ...), custom_call_target="tpu_custom_call" | custom-call | flops 1610612736 | bytes 6553600 | tf_op jit(solution)/shard_map/wgrad_qkv/pallas_call | solution.py:562
  278.3 5.3 %collective-permute-done.42 = bf16[2,128,640]{2,1,0:T(8,128)(2,1)S(1)} collective-permute-done((bf16[2,128,640]{2,1,0:T(8,128)(2,1)S(1)}, bf16[2,128,640]{2,1,0:T(8,128)(2,1)S(1)}, u32[]{:S(2)}, u32[]{:S(2)}) %collective-permute-start.42) | collective-permute-done | bytes 327712 | tf_op jit(solution)/shard_map/ppermute | solution.py:51
  288.9 12.7 %collective-permute-done.45 = bf16[2,128,640]{2,1,0:T(8,128)(2,1)S(1)} collective-permute-done((bf16[2,128,640]{2,1,0:T(8,128)(2,1)S(1)}, bf16[2,128,640]{2,1,0:T(8,128)(2,1)S(1)}, u32[]{:S(2)}, u32[]{:S(2)}) %collective-permute-start.45) | collective-permute-done | bytes 327712 | tf_op jit(solution)/shard_map/ppermute | solution.py:51
  307.9 7.8 %collective-permute-done.47 = bf16[2,128,640]{2,1,0:T(8,128)(2,1)S(1)} collective-permute-done((bf16[2,128,640]{2,1,0:T(8,128)(2,1)S(1)}, bf16[2,128,640]{2,1,0:T(8,128)(2,1)S(1)}, u32[]{:S(2)}, u32[]{:S(2)}) %collective-permute-start.47) | collective-permute-done | bytes 327712 | tf_op jit(solution)/shard_map/ppermute | solution.py:51
  315.9 4.9 %collective-permute-done.50.s_ref = bf16[4,704,128]{2,1,0:T(8,128)(2,1)S(1)} collective-permute-done((bf16[4,704,128]{2,1,0:T(8,128)(2,1)S(1)}, bf16[4,704,128]{2,1,0:T(8,128)(2,1)S(1)}, u32[]{:S(2)}, u32[]{:S(2)}) %collective-permute-start.50) | collective-permute-done | bytes 720928 | tf_op jit(solution)/shard_map/ppermute | solution.py:51
  323.3 4.4 %collective-permute-done.55 = bf16[2,704,128]{2,1,0:T(8,128)(2,1)S(1)} collective-permute-done((bf16[2,704,128]{2,1,0:T(8,128)(2,1)S(1)}, bf16[2,704,128]{2,1,0:T(8,128)(2,1)S(1)}, u32[]{:S(2)}, u32[]{:S(2)}) %collective-permute-start.55) | collective-permute-done | bytes 360480 | tf_op jit(solution)/shard_map/ppermute | solution.py:51
  337.7 7.4 %collective-permute-done.56.s_ref = bf16[4,704,128]{2,1,0:T(8,128)(2,1)S(1)} collective-permute-done((bf16[4,704,128]{2,1,0:T(8,128)(2,1)S(1)}, bf16[4,704,128]{2,1,0:T(8,128)(2,1)S(1)}, u32[]{:S(2)}, u32[]{:S(2)}) %collective-permute-start.56) | collective-permute-done | bytes 720928 | tf_op jit(solution)/shard_map/ppermute | solution.py:51
  348.6 4.7 %collective-permute-done.54 = f32[1,1024]{1,0:T(1,128)S(1)} collective-permute-done((f32[1,1024]{1,0:T(1,128)S(1)}, f32[1,1024]{1,0:T(1,128)S(1)}, u32[]{:S(2)}, u32[]{:S(2)}) %collective-permute-start.54) | collective-permute-done | bytes 4128 | tf_op jit(solution)/shard_map/ppermute | solution.py:51
  (311 shorter events, 134.3 us)
Async XLA Ops:
  3.5 26.3 %collective-permute-start = (bf16[512,1024]{1,0:T(8,128)(2,1)S(1)}, bf16[512,1024]{1,0:T(8,128)(2,1)S(1)}, u32[]{:S(2)}, u32[]{:S(2)}) collective-permute-start(bf16[512,1024]{1,0:T(8,128)(2,1)S(1)} %norm.1.a_ref.n0), channel_id=1, source_target_pairs={{0,2},{1,3},{2,0},{3,1},{4,6},{5,7},{6,4},{7,5},{8,10},{9,11},{10,... | collective-permute-start | bytes 3145736 | tf_op jit(solution)/shard_map/ppermute | solution.py:51
  30.5 30.9 %collective-permute-start.4 = (bf16[256,1024]{1,0:T(8,128)(2,1)S(1)}, bf16[256,1024]{1,0:T(8,128)(2,1)S(1)}, u32[]{:S(2)}, u32[]{:S(2)}) collective-permute-start(bf16[256,1024]{1,0:T(8,128)(2,1)S(1)} %copy-done.8), channel_id=1, source_target_pairs={{0,2},{1,3},{2,0},{3,1},{4,6},{5,7},{6,4},{7,5},{8,10},{9,11},{10,... | collective-permute-start | bytes 1572872 | tf_op jit(solution)/shard_map/ppermute | solution.py:51
  32.6 45.6 %collective-permute-start.3 = (bf16[512,1024]{1,0:T(8,128)(2,1)}, bf16[512,1024]{1,0:T(8,128)(2,1)S(1)}, u32[]{:S(2)}, u32[]{:S(2)}) collective-permute-start(bf16[512,1024]{1,0:T(8,128)(2,1)} %cot.1), channel_id=1, source_target_pairs={{0,2},{1,3},{2,0},{3,1},{4,6},{5,7},{6,4},{7,5},{8,10},{9,11},{10,... | collective-permute-start | bytes 3145736 | tf_op jit(solution)/shard_map/ppermute | solution.py:51
  81.7 25.4 %collective-permute-start.10 = (bf16[512,1024]{1,0:T(8,128)(2,1)S(1)}, bf16[512,1024]{1,0:T(8,128)(2,1)S(1)}, u32[]{:S(2)}, u32[]{:S(2)}) collective-permute-start(bf16[512,1024]{1,0:T(8,128)(2,1)S(1)} %get-tuple-element.172.na.c0), channel_id=1, source_target_pairs={{0,2},{1,3},{2,0},{3,1},{4,6},{5,7},{6,4},{7,5},{8,10},{9,11},{10,... | collective-permute-start | bytes 3145736 | tf_op jit(solution)/shard_map/ppermute | solution.py:51
  83.4 24.2 %collective-permute-start.16 = (bf16[512,1024]{1,0:T(8,128)(2,1)S(1)}, bf16[512,1024]{1,0:T(8,128)(2,1)S(1)}, u32[]{:S(2)}, u32[]{:S(2)}) collective-permute-start(bf16[512,1024]{1,0:T(8,128)(2,1)S(1)} %collective-permute-done.3.ca.c2), channel_id=1, source_target_pairs={{0,1},{1,0},{2,3},{3,2},{4,5},{5,4},{6,7},{7,6},{8,9},{9,8},{10,11... | collective-permute-start | bytes 3145736 | tf_op jit(solution)/shard_map/ppermute | solution.py:51
  107.1 27.9 %collective-permute-start.13 = (bf16[512,1024]{1,0:T(8,128)(2,1)S(1)}, bf16[512,1024]{1,0:T(8,128)(2,1)S(1)}, u32[]{:S(2)}, u32[]{:S(2)}) collective-permute-start(bf16[512,1024]{1,0:T(8,128)(2,1)S(1)} %get-tuple-element.181), channel_id=1, source_target_pairs={{0,1},{1,0},{2,3},{3,2},{4,5},{5,4},{6,7},{7,6},{8,9},{9,8},{10,11... | collective-permute-start | bytes 3145736 | tf_op jit(solution)/shard_map/ppermute | solution.py:51
  107.6 27.4 %collective-permute-start.14 = (bf16[512,1024]{1,0:T(8,128)(2,1)S(1)}, bf16[512,1024]{1,0:T(8,128)(2,1)S(1)}, u32[]{:S(2)}, u32[]{:S(2)}) collective-permute-start(bf16[512,1024]{1,0:T(8,128)(2,1)S(1)} %get-tuple-element.182), channel_id=1, source_target_pairs={{0,1},{1,0},{2,3},{3,2},{4,5},{5,4},{6,7},{7,6},{8,9},{9,8},{10,11... | collective-permute-start | bytes 3145736 | tf_op jit(solution)/shard_map/ppermute | solution.py:51
  139.1 34.2 %collective-permute-start.18 = (bf16[512,1024]{1,0:T(8,128)(2,1)}, bf16[512,1024]{1,0:T(8,128)(2,1)}, u32[]{:S(2)}, u32[]{:S(2)}) collective-permute-start(bf16[512,1024]{1,0:T(8,128)(2,1)} %get-tuple-element.192), channel_id=1, source_target_pairs={{0,1},{1,0},{2,3},{3,2},{4,5},{5,4},{6,7},{7,6},{8,9},{9,8},{10,11... | collective-permute-start | bytes 3145736 | tf_op jit(solution)/shard_map/ppermute | solution.py:51
  139.3 35.6 %collective-permute-start.19 = (bf16[512,1024]{1,0:T(8,128)(2,1)}, bf16[512,1024]{1,0:T(8,128)(2,1)S(1)}, u32[]{:S(2)}, u32[]{:S(2)}) collective-permute-start(bf16[512,1024]{1,0:T(8,128)(2,1)} %add_convert_fusion.2), channel_id=1, source_target_pairs={{0,2},{1,3},{2,0},{3,1},{4,6},{5,7},{6,4},{7,5},{8,10},{9,11},{10,... | collective-permute-start | bytes 3145736 | tf_op jit(solution)/shard_map/ppermute | solution.py:51
  157.6 28.4 %collective-permute-start.24 = (bf16[4,704,128]{2,1,0:T(8,128)(2,1)S(1)}, bf16[4,704,128]{2,1,0:T(8,128)(2,1)S(1)}, u32[]{:S(2)}, u32[]{:S(2)}) collective-permute-start(bf16[4,704,128]{2,1,0:T(8,128)(2,1)S(1)} %get-tuple-element.216), channel_id=1, source_target_pairs={{0,4},{4,0},{8,12},{12,8},{16,20},{20,16},{24,28},{28,24},{1,5},{5... | collective-permute-start | bytes 2162696 | tf_op jit(solution)/shard_map/ppermute | solution.py:51
  186.9 38.4 %collective-permute-start.30 = (bf16[4,704,128]{2,1,0:T(8,128)(2,1)S(1)}, bf16[4,704,128]{2,1,0:T(8,128)(2,1)S(1)}, u32[]{:S(2)}, u32[]{:S(2)}) collective-permute-start(bf16[4,704,128]{2,1,0:T(8,128)(2,1)S(1)} %get-tuple-element.237), channel_id=1, source_target_pairs={{0,8},{4,12},{8,0},{12,4},{16,24},{20,28},{24,16},{28,20},{1,9},{5... | collective-permute-start | bytes 2162696 | tf_op jit(solution)/shard_map/ppermute | solution.py:51
  195.2 25.6 %collective-permute-start.29 = (bf16[2,704,128]{2,1,0:T(8,128)(2,1)S(1)}, bf16[2,704,128]{2,1,0:T(8,128)(2,1)S(1)}, u32[]{:S(2)}, u32[]{:S(2)}) collective-permute-start(bf16[2,704,128]{2,1,0:T(8,128)(2,1)S(1)} %get-tuple-element.220), channel_id=1, source_target_pairs={{0,8},{4,12},{8,0},{12,4},{16,24},{20,28},{24,16},{28,20},{1,9},{5... | collective-permute-start | bytes 1081352 | tf_op jit(solution)/shard_map/ppermute | solution.py:51
  197.3 23.6 %collective-permute-start.28 = (bf16[2,704,128]{2,1,0:T(8,128)(2,1)S(1)}, bf16[2,704,128]{2,1,0:T(8,128)(2,1)S(1)}, u32[]{:S(2)}, u32[]{:S(2)}) collective-permute-start(bf16[2,704,128]{2,1,0:T(8,128)(2,1)S(1)} %add_convert_fusion.9), channel_id=1, source_target_pairs={{0,16},{4,20},{8,24},{12,28},{16,0},{20,4},{24,8},{28,12},{1,17},{... | collective-permute-start | bytes 1081352 | tf_op jit(solution)/shard_map/ppermute | solution.py:51
  200.1 27.0 %collective-permute-start.31 = (bf16[256,1024]{1,0:T(8,128)(2,1)S(1)}, bf16[256,1024]{1,0:T(8,128)(2,1)S(1)}, u32[]{:S(2)}, u32[]{:S(2)}) collective-permute-start(bf16[256,1024]{1,0:T(8,128)(2,1)S(1)} %add_convert_fusion.3.rest_0_), channel_id=1, source_target_pairs={{0,2},{1,3},{2,0},{3,1},{4,6},{5,7},{6,4},{7,5},{8,10},{9,11},{10,... | collective-permute-start | bytes 1572872 | tf_op jit(solution)/shard_map/ppermute | solution.py:51
  221.1 29.3 %collective-permute-start.35 = (bf16[2,704,128]{2,1,0:T(8,128)(2,1)S(1)}, bf16[2,704,128]{2,1,0:T(8,128)(2,1)S(1)}, u32[]{:S(2)}, u32[]{:S(2)}) collective-permute-start(bf16[2,704,128]{2,1,0:T(8,128)(2,1)S(1)} %get-tuple-element.294), channel_id=1, source_target_pairs={{0,16},{4,20},{8,24},{12,28},{16,0},{20,4},{24,8},{28,12},{1,17},{... | collective-permute-start | bytes 1081352 | tf_op jit(solution)/shard_map/ppermute | solution.py:51
  223.6 26.8 %collective-permute-start.34 = (bf16[2,704,128]{2,1,0:T(8,128)(2,1)S(1)}, bf16[2,704,128]{2,1,0:T(8,128)(2,1)S(1)}, u32[]{:S(2)}, u32[]{:S(2)}) collective-permute-start(bf16[2,704,128]{2,1,0:T(8,128)(2,1)S(1)} %get-tuple-element.295), channel_id=1, source_target_pairs={{0,8},{4,12},{8,0},{12,4},{16,24},{20,28},{24,16},{28,20},{1,9},{5... | collective-permute-start | bytes 1081352 | tf_op jit(solution)/shard_map/ppermute | solution.py:51
  225.5 25.1 %collective-permute-start.36 = (bf16[2,704,128]{2,1,0:T(8,128)(2,1)S(1)}, bf16[2,704,128]{2,1,0:T(8,128)(2,1)S(1)}, u32[]{:S(2)}, u32[]{:S(2)}) collective-permute-start(bf16[2,704,128]{2,1,0:T(8,128)(2,1)S(1)} %get-tuple-element.239), channel_id=1, source_target_pairs={{0,4},{4,0},{8,12},{12,8},{16,20},{20,16},{24,28},{28,24},{1,5},{5... | collective-permute-start | bytes 1081352 | tf_op jit(solution)/shard_map/ppermute | solution.py:51
  231.8 24.3 %collective-permute-start.32 = (bf16[512,1024]{1,0:T(8,128)(2,1)S(1)}, bf16[512,1024]{1,0:T(8,128)(2,1)S(1)}, u32[]{:S(2)}, u32[]{:S(2)}) collective-permute-start(bf16[512,1024]{1,0:T(8,128)(2,1)S(1)} %add_convert_fusion.1), channel_id=1, source_target_pairs={{0,2},{1,3},{2,0},{3,1},{4,6},{5,7},{6,4},{7,5},{8,10},{9,11},{10,... | collective-permute-start | bytes 3145736 | tf_op jit(solution)/shard_map/ppermute | solution.py:51
  258.4 28.5 %collective-permute-start.46 = (bf16[4,704,128]{2,1,0:T(8,128)(2,1)S(1)}, bf16[4,704,128]{2,1,0:T(8,128)(2,1)S(1)}, u32[]{:S(2)}, u32[]{:S(2)}) collective-permute-start(bf16[4,704,128]{2,1,0:T(8,128)(2,1)S(1)} %pad_maximum_fusion.k_ref), channel_id=1, source_target_pairs={{0,4},{4,0},{8,12},{12,8},{16,20},{20,16},{24,28},{28,24},{1,5},{5... | collective-permute-start | bytes 2162696 | tf_op jit(solution)/shard_map/ppermute | solution.py:51
  259.9 23.7 %collective-permute-start.41 = (bf16[2,704,128]{2,1,0:T(8,128)(2,1)S(1)}, bf16[2,704,128]{2,1,0:T(8,128)(2,1)S(1)}, u32[]{:S(2)}, u32[]{:S(2)}) collective-permute-start(bf16[2,704,128]{2,1,0:T(8,128)(2,1)S(1)} %add_convert_fusion.5), channel_id=1, source_target_pairs={{0,16},{4,20},{8,24},{12,28},{16,0},{20,4},{24,8},{28,12},{1,17},{... | collective-permute-start | bytes 1081352 | tf_op jit(solution)/shard_map/ppermute | solution.py:51
  265.5 40.3 %collective-permute-start.39 = (bf16[512,1024]{1,0:T(8,128)(2,1)S(1)}, bf16[512,1024]{1,0:T(8,128)(2,1)S(1)}, u32[]{:S(2)}, u32[]{:S(2)}) collective-permute-start(bf16[512,1024]{1,0:T(8,128)(2,1)S(1)} %add_convert_fusion), channel_id=1, source_target_pairs={{0,2},{1,3},{2,0},{3,1},{4,6},{5,7},{6,4},{7,5},{8,10},{9,11},{10,... | collective-permute-start | bytes 3145736 | tf_op jit(solution)/shard_map/ppermute | solution.py:51
  305.2 22.5 %collective-permute-start.55 = (bf16[2,704,128]{2,1,0:T(8,128)(2,1)S(1)}, bf16[2,704,128]{2,1,0:T(8,128)(2,1)S(1)}, u32[]{:S(2)}, u32[]{:S(2)}) collective-permute-start(bf16[2,704,128]{2,1,0:T(8,128)(2,1)S(1)} %add_convert_fusion.4), channel_id=1, source_target_pairs={{0,4},{4,0},{8,12},{12,8},{16,20},{20,16},{24,28},{28,24},{1,5},{5... | collective-permute-start | bytes 1081352 | tf_op jit(solution)/shard_map/ppermute | solution.py:51
  329.5 24.4 %collective-permute-start.60 = (bf16[4,128,640]{2,1,0:T(8,128)(2,1)S(1)}, bf16[4,128,640]{2,1,0:T(8,128)(2,1)S(1)}, u32[]{:S(2)}, u32[]{:S(2)}) collective-permute-start(bf16[4,128,640]{2,1,0:T(8,128)(2,1)S(1)} %pad_maximum_fusion.3.a_ref.ak), channel_id=1, source_target_pairs={{0,4},{4,0},{8,12},{12,8},{16,20},{20,16},{24,28},{28,24},{1,5},{5... | collective-permute-start | bytes 1966088 | tf_op jit(solution)/shard_map/ppermute | solution.py:51
  331.0 22.9 %collective-permute-start.61 = (bf16[4,128,384]{2,1,0:T(8,128)(2,1)S(1)}, bf16[4,128,384]{2,1,0:T(8,128)(2,1)S(1)}, u32[]{:S(2)}, u32[]{:S(2)}) collective-permute-start(bf16[4,128,384]{2,1,0:T(8,128)(2,1)S(1)} %pad_maximum_fusion.4.b_ref.bk), channel_id=1, source_target_pairs={{0,4},{4,0},{8,12},{12,8},{16,20},{20,16},{24,28},{28,24},{1,5},{5... | collective-permute-start | bytes 1179656 | tf_op jit(solution)/shard_map/ppermute | solution.py:51
  (118 other events, 1175.3 us)
